TPU v7x, 128 devices: a whole 4x4x4 slice. The times are simulated.
128 devices in a mesh: dp: 8 (over y_hi, x), width: 4 (over y_lo, core), heads: 4 (over z).
Axes of the slice: x: 4, y: 4 (y_hi: 2, y_lo: 2; y = y_hi * 2 + y_lo), z: 4, core: 2. Of those that a mesh axis runs over, the one named last changes fastest.
Arguments:
- tokens: bfloat16 [16384, 1280], P(('dp', 'heads'), 'width'), may hold values from -22 to 22
- ln_gain: float32 [2, 1280], P(None, 'width'), may hold values from 0.5 to 1.5
- ln_bias: float32 [2, 1280], P(None, 'width'), may hold values from -4 to 4
- w_attn: bfloat16 [3, 1280, 1280], P(None, 'width', 'heads'), may hold values from -0.15625 to 0.15625
- b_qv: float32 [2, 1280], P(None, 'heads'), may hold values from -4 to 4
- w_proj: bfloat16 [1280, 1280], P('heads', 'width'), may hold values from -1.25 to 1.25
- b_proj: float32 [1280], P('width'), may hold values from -4 to 4
- w_fc: bfloat16 [1280, 5120], P('width', 'heads'), may hold values from -1 to 1
- b_fc: float32 [5120], P('heads'), may hold values from -4 to 4
- w_out: bfloat16 [5120, 1280], P('heads', 'width'), may hold values from -0.078125 to 0.078125
- b_out: float32 [1280], P('width'), may hold values from -4 to 4
- d_out: bfloat16 [16384, 1280], P(('dp', 'heads'), 'width'), may hold values from -22 to 22
Outputs:
- block_out: bfloat16 [16384, 1280], P(('dp', 'heads'), 'width')
- d_tokens: bfloat16 [16384, 1280], P(('dp', 'heads'), 'width')
- d_ln_gain: float32 [2, 1280], P(None, 'width')
- d_ln_bias: float32 [2, 1280], P(None, 'width')
- d_w_attn: float32 [3, 1280, 1280], P(None, 'width', 'heads')
- d_b_qv: float32 [2, 1280], P(None, 'heads')
- d_w_proj: float32 [1280, 1280], P('heads', 'width')
- d_b_proj: float32 [1280], P('width')
- d_w_fc: float32 [1280, 5120], P('width', 'heads')
- d_b_fc: float32 [5120], P('heads')
- d_w_out: float32 [5120, 1280], P('heads', 'width')
- d_b_out: float32 [1280], P('width')
All inputs are finite; a program needn't handle non-finite values.
Results may differ from a plain program's by a relative error of at most 0.023.
Values may be sent and summed in bfloat16 or wider, within the bound.
A program may use at most 192 MiB of HBM per device.

v0:
```python
import jax
import jax.numpy as jnp
from jax import lax
from jax.sharding import PartitionSpec as P

HS = 64
LEN = 2048


EPSILON = 1e-05
GELU_COEF = 0.7978845608028654
MASKED = -1e30


def copy_for_each(shard, axis):
    copies = jnp.broadcast_to(shard, (lax.axis_size(axis), *shard.shape))
    return lax.all_to_all(copies, axis, split_axis=0, concat_axis=0, tiled=True)


def in_order(pieces, dim):
    lengths = list(pieces.shape[1:])
    lengths[dim] *= pieces.shape[0]
    return jnp.moveaxis(pieces, 0, dim).reshape(lengths)


def gather_directly(shard, axis, dim):
    pieces = copy_for_each(shard, axis)
    return in_order(pieces, dim)


def cut_along(shard, dim, count):
    before, after = (shard.shape[:dim], shard.shape[dim + 1 :])
    return jnp.moveaxis(shard.reshape(*before, count, -1, *after), dim, 0)


def sum_at_owner(shard, axis, dim):
    pieces = cut_along(shard, dim, lax.axis_size(axis))
    arrived = lax.all_to_all(pieces, axis, split_axis=0, concat_axis=0, tiled=True)
    return arrived.astype(jnp.float32).sum(axis=0)


def of_everyone(shard, axis):
    return copy_for_each(shard, axis).sum(axis=0)


def together(arrays, axis):
    ravelled, at, gathered = (jnp.concatenate([a.reshape(-1) for a in arrays]), 0, [])
    subtotal = of_everyone(ravelled, axis)
    for a in arrays:
        gathered.append(subtotal[at : at + a.size].reshape(a.shape))
        at += a.size
    return tuple(gathered)


def gelu_tanh(inputs):
    return (
        0.5 * inputs * (1.0 + jnp.tanh(GELU_COEF * (inputs + 0.044715 * inputs * inputs * inputs)))
    )


def dot_rows(left_side, right_side):
    return jnp.dot(left_side, right_side, preferred_element_type=jnp.float32)


def dot_back(left_side, right_side):
    return lax.dot_general(
        left_side, right_side, (((1,), (1,)), ((), ())), preferred_element_type=jnp.float32
    )


def dot_front(left_side, right_side):
    return lax.dot_general(
        left_side, right_side, (((0,), (0,)), ((), ())), preferred_element_type=jnp.float32
    )


def heads_rows(local_part):
    return gather_directly(local_part, "heads", 0)


def width_rows(local_part):
    return lax.all_gather(local_part, "width", axis=0, tiled=True)


def sum_width(gathered, weight, multiply):
    row_count = gathered.shape[0] // lax.axis_size("width")

    def partial_term(offset, amount):
        return multiply(gathered, weight)

    return lax.psum_scatter(
        partial_term(jnp.int32(0), row_count * lax.axis_size("width")),
        "width",
        scatter_dimension=0,
        tiled=True,
    )


def sum_heads(gathered, weight, multiply):
    row_count = gathered.shape[0] // lax.axis_size("heads")

    def partial_term(offset, amount):
        return multiply(gathered, weight)

    return sum_at_owner(
        partial_term(jnp.int32(0), row_count * lax.axis_size("heads")).astype(jnp.bfloat16),
        "heads",
        0,
    )


def hidden_sum(gathered, weight, multiply):
    return sum_width(gathered, weight, multiply)


def hidden_rows(local_part):
    return width_rows(local_part)


def norm_forward(values, gain_row, shift_row):
    full_width = values.shape[1] * lax.axis_size("width")
    row_total, row_squares = together(
        (jnp.sum(values, axis=1, keepdims=True), jnp.sum(values * values, axis=1, keepdims=True)),
        "width",
    )
    row_mean = row_total / full_width
    centred = values - row_mean
    spread = row_squares / full_width - row_mean * row_mean
    norm_scale = lax.rsqrt(spread + EPSILON)
    unit_rows = centred * norm_scale
    return (unit_rows, norm_scale, (unit_rows * gain_row + shift_row).astype(jnp.bfloat16))


def norm_backward(grad_normed, unit_rows, norm_scale, gain_row):
    full_width = grad_normed.shape[1] * lax.axis_size("width")
    scaled = grad_normed * gain_row
    row_total, row_along = together(
        (
            jnp.sum(scaled, axis=1, keepdims=True),
            jnp.sum(scaled * unit_rows, axis=1, keepdims=True),
        ),
        "width",
    )
    return norm_scale * (scaled - row_total / full_width - unit_rows * (row_along / full_width))


def block_size():
    return 512


def window_scores(query_block, key_part, block_start, window_start):
    scores = jnp.einsum(
        "qhd,khd->hqk", query_block, key_part, preferred_element_type=jnp.float32
    ) * HS ** (-0.5)
    query_place = block_start + lax.iota(jnp.int32, query_block.shape[0])
    key_place = window_start + lax.iota(jnp.int32, key_part.shape[0])
    visible = key_place[None, :] <= query_place[:, None]
    return jnp.where(visible[None], scores, MASKED)


def split_window(kv_all, head_cols, heads_here):
    key_part = kv_all[:, :head_cols].reshape(LEN, heads_here, HS)
    value_part = kv_all[:, head_cols:].reshape(LEN, heads_here, HS)
    return (key_part, value_part)


def attend(queries, kv_all, first_row):
    row_count, head_cols = queries.shape
    heads_here = head_cols // HS
    block_rows = block_size()

    def one_block(running, step_index):
        block_start = first_row + step_index * block_rows
        window_start = block_start // LEN * LEN
        query_block = queries.reshape(block_rows, heads_here, HS)
        key_part, value_part = split_window(kv_all, head_cols, heads_here)
        scores = window_scores(query_block, key_part, block_start, window_start)
        row_peak = jnp.max(scores, axis=-1, keepdims=True)
        weights = jnp.exp(scores - row_peak)
        row_total = jnp.sum(weights, axis=-1, keepdims=True)
        normalized_low = (weights / row_total).astype(jnp.bfloat16)
        result = jnp.einsum(
            "hqk,khd->qhd", normalized_low, value_part, preferred_element_type=jnp.float32
        )
        return (
            running,
            (
                result.reshape(block_rows, head_cols).astype(jnp.bfloat16),
                (row_peak + jnp.log(row_total))[..., 0],
            ),
        )

    _, (outputs, log_totals) = lax.scan(
        one_block, 0, jnp.arange(row_count // block_rows, dtype=jnp.int32)
    )
    return (outputs.reshape(row_count, head_cols), log_totals)


def attend_back(queries, kv_all, log_totals, grad_attended, first_row):
    row_count, head_cols = queries.shape
    heads_here = head_cols // HS
    block_rows = block_size()
    factor = HS ** (-0.5)

    def one_block(running, inputs):
        step_index, log_block = inputs
        block_start = first_row + step_index * block_rows
        window_start = block_start // LEN * LEN
        query_block = queries.reshape(block_rows, heads_here, HS)
        grad_block = grad_attended.reshape(block_rows, heads_here, HS)
        key_part, value_part = split_window(kv_all, head_cols, heads_here)
        scores = window_scores(query_block, key_part, block_start, window_start)
        normalized = jnp.exp(scores - log_block[..., None])
        normalized_low = normalized.astype(jnp.bfloat16)
        grad_probs = jnp.einsum(
            "qhd,khd->hqk", grad_block, value_part, preferred_element_type=jnp.float32
        )
        row_inner = jnp.sum(grad_probs * normalized, axis=-1, keepdims=True)
        grad_scores = (normalized * (grad_probs - row_inner)).astype(jnp.bfloat16)
        grad_query = (
            jnp.einsum("hqk,khd->qhd", grad_scores, key_part, preferred_element_type=jnp.float32)
            * factor
        )
        grad_key = (
            jnp.einsum("hqk,qhd->khd", grad_scores, query_block, preferred_element_type=jnp.float32)
            * factor
        )
        grad_value = jnp.einsum(
            "hqk,qhd->khd", normalized_low, grad_block, preferred_element_type=jnp.float32
        )
        update = jnp.concatenate(
            (grad_key.reshape(LEN, head_cols), grad_value.reshape(LEN, head_cols)), 1
        )
        current = running
        running = current + update
        return (running, grad_query.reshape(block_rows, head_cols))

    initial = jnp.zeros(kv_all.shape, jnp.float32)
    grad_window, grad_queries = lax.scan(
        one_block, initial, (jnp.arange(row_count // block_rows, dtype=jnp.int32), log_totals)
    )
    return (grad_queries.reshape(row_count, head_cols), grad_window)


def shards(tokens, ln_gain, ln_bias, w_attn, b_qv, w_proj, b_proj, w_fc, b_fc, w_out, b_out, d_out):
    source = tokens.astype(jnp.float32)
    unit_first, scale_first, normed1 = norm_forward(source, ln_gain[0], ln_bias[0])
    normed1_all = heads_rows(normed1)
    w_joined = jnp.concatenate((w_attn[0], w_attn[1], w_attn[2]), 1)
    mixed = sum_width(normed1_all, w_joined, dot_rows)
    head_cols = w_attn.shape[2]
    queries = (mixed[:, :head_cols] + b_qv[0]).astype(jnp.bfloat16)
    key_rows = mixed[:, head_cols : 2 * head_cols].astype(jnp.bfloat16)
    value_rows = (mixed[:, 2 * head_cols :] + b_qv[1]).astype(jnp.bfloat16)
    first_row = lax.axis_index("width") * queries.shape[0]
    kv_all = gather_directly(jnp.concatenate((key_rows, value_rows), 1), "width", 0)
    attended, log_totals = attend(queries, kv_all, first_row)
    attended_all = width_rows(attended)
    middle = source + sum_heads(attended_all, w_proj, dot_rows) + b_proj
    unit_second, scale_second, normed2 = norm_forward(middle, ln_gain[1], ln_bias[1])
    normed2_all = heads_rows(normed2)
    pre = hidden_sum(normed2_all, w_fc, dot_rows) + b_fc
    hidden_all = hidden_rows(gelu_tanh(pre).astype(jnp.bfloat16))
    block_out = (middle + sum_heads(hidden_all, w_out, dot_rows) + b_out).astype(jnp.bfloat16)
    grad_all = heads_rows(d_out)
    d_w_out = dot_front(hidden_all, grad_all)
    d_b_out = jnp.sum(grad_all, axis=0, dtype=jnp.float32)
    grad_hidden = hidden_sum(grad_all, w_out, dot_back)
    grad_pre = jax.vjp(gelu_tanh, pre)[1](grad_hidden)[0].astype(jnp.bfloat16)
    grad_pre_all = hidden_rows(grad_pre)
    d_w_fc = dot_front(normed2_all, grad_pre_all)
    d_b_fc = jnp.sum(grad_pre_all, axis=0, dtype=jnp.float32)
    grad_normed2 = sum_heads(grad_pre_all, w_fc, dot_back)
    grad_middle = d_out.astype(jnp.float32) + norm_backward(
        grad_normed2, unit_second, scale_second, ln_gain[1]
    )
    grad_branch_all = heads_rows(grad_middle.astype(jnp.bfloat16))
    d_w_proj = dot_front(attended_all, grad_branch_all)
    d_b_proj = jnp.sum(grad_branch_all, axis=0, dtype=jnp.float32)
    grad_attended = sum_width(grad_branch_all, w_proj, dot_back).astype(jnp.bfloat16)
    grad_queries, grad_window = attend_back(queries, kv_all, log_totals, grad_attended, first_row)
    grad_kv = sum_at_owner(grad_window.astype(jnp.bfloat16), "width", 0)
    grad_mixed = jnp.concatenate((grad_queries, grad_kv), 1).astype(jnp.bfloat16)
    grad_mixed_all = width_rows(grad_mixed)
    d_joined = dot_front(normed1_all, grad_mixed_all)
    mixed_sums = jnp.sum(grad_mixed_all, axis=0, dtype=jnp.float32)
    d_b_qv = jnp.stack((mixed_sums[:head_cols], mixed_sums[2 * head_cols :]))
    grad_normed1 = sum_heads(grad_mixed_all, w_joined, dot_back)
    d_tokens = (
        grad_middle + norm_backward(grad_normed1, unit_first, scale_first, ln_gain[0])
    ).astype(jnp.bfloat16)
    d_w_attn = d_joined.reshape(d_joined.shape[0], 3, head_cols).transpose(1, 0, 2)
    d_gain_local = jnp.stack(
        (jnp.sum(grad_normed1 * unit_first, axis=0), jnp.sum(grad_normed2 * unit_second, axis=0))
    )
    d_shift_local = jnp.stack((jnp.sum(grad_normed1, axis=0), jnp.sum(grad_normed2, axis=0)))
    d_w_attn, d_b_qv, d_w_proj, d_b_proj, d_w_fc, d_b_fc, d_w_out, d_b_out = (
        lax.psum(d_w_attn.astype(jnp.bfloat16), "dp").astype(jnp.float32),
        lax.psum(d_b_qv.astype(jnp.bfloat16), "dp").astype(jnp.float32),
        lax.psum(d_w_proj.astype(jnp.bfloat16), "dp").astype(jnp.float32),
        lax.psum(d_b_proj.astype(jnp.bfloat16), "dp").astype(jnp.float32),
        lax.psum(d_w_fc.astype(jnp.bfloat16), "dp").astype(jnp.float32),
        lax.psum(d_b_fc.astype(jnp.bfloat16), "dp").astype(jnp.float32),
        lax.psum(d_w_out.astype(jnp.bfloat16), "dp").astype(jnp.float32),
        lax.psum(d_b_out.astype(jnp.bfloat16), "dp").astype(jnp.float32),
    )
    d_ln_gain, d_ln_bias = together((d_gain_local, d_shift_local), ("dp", "heads"))
    return (
        block_out,
        d_tokens,
        d_ln_gain,
        d_ln_bias,
        d_w_attn,
        d_b_qv,
        d_w_proj,
        d_b_proj,
        d_w_fc,
        d_b_fc,
        d_w_out,
        d_b_out,
    )


def solution(mesh):
    in_specs = (
        P(("dp", "heads"), "width"),
        P(None, "width"),
        P(None, "width"),
        P(None, "width", "heads"),
        P(None, "heads"),
        P("heads", "width"),
        P("width"),
        P("width", "heads"),
        P("heads"),
        P("heads", "width"),
        P("width"),
        P(("dp", "heads"), "width"),
    )
    out_specs = (
        P(("dp", "heads"), "width"),
        P(("dp", "heads"), "width"),
        P(None, "width"),
        P(None, "width"),
        P(None, "width", "heads"),
        P(None, "heads"),
        P("heads", "width"),
        P("width"),
        P("width", "heads"),
        P("heads"),
        P("heads", "width"),
        P("width"),
    )
    return jax.shard_map(shards, mesh=mesh, in_specs=in_specs, out_specs=out_specs, check_vma=False)
```

profile of v0, /device:TPU:0, one launch (start us, length us, event | category | flops | bytes accessed | tf_op | source)
XLA Modules:
  0.0 846.2 jit_solution(7077456396550878691)
XLA Ops:
  25.1 16.6 %all-to-all-done.1 = bf16[4,512,320]{1,2,0:T(8,128)(2,1)S(1)} async-done(((bf16[4,512,320]{1,2,0:T(8,128)(2,1)}), bf16[4,512,320]{1,2,0:T(8,128)(2,1)S(1)}, u32[]{:S(2)}, u32[]{:S(2)}) %all-to-all-start.1) | async-done | bytes 1310752 | tf_op jit(solution)/shard_map/all_to_all | solution.py:17
  47.9 74.3 %reduce-scatter.5.cloned.1.call-done = f32[512,960]{0,1:T(8,128)} async-done(((f32[2048,960]{0,1:T(8,128)}), f32[512,960]{0,1:T(8,128)}) %reduce-scatter.5.cloned.1.call-update) | async-done | bytes 1966096 | tf_op jit(solution)/shard_map/reduce_scatter | solution.py:91
  133.8 29.4 %all-to-all-done.2 = bf16[4,512,640]{1,2,0:T(8,128)(2,1)} async-done(((bf16[4,512,640]{1,2,0:T(8,128)(2,1)}), bf16[4,512,640]{1,2,0:T(8,128)(2,1)}, u32[]{:S(2)}, u32[]{:S(2)}) %all-to-all-start.2) | async-done | bytes 2621472 | tf_op jit(solution)/shard_map/all_to_all | solution.py:17
  184.5 9.6 %fusion.22 = bf16[5,64,512]{2,1,0:T(8,128)(2,1)} fusion(bf16[2048,5,64]{0,2,1:T(8,128)(2,1)S(1)} %bitcast.98, f32[5,512,2048]{2,1,0:T(8,128)} %copy-done.2, f32[5,512]{1,0:T(8,128)S(1)} %fusion, f32[5,512]{1,0:T(8,128)S(1)} %get-tuple-element.106), kind=kOutput, calls=%fused_computation.49 | convolution fusion | flops 686981120 | bytes 22630400 | tf_op jit(solution)/shard_map/while/body/eval_jaxpr/hqk,khd->qhd/dot_general | solution.py:182
  195.3 22.1 %all_to_all.80 = bf16[4,512,320]{1,2,0:T(8,128)(2,1)S(1)} all-to-all(bf16[4,512,320]{1,2,0:T(8,128)(2,1)S(1)} %broadcast_in_dim.97), channel_id=1, replica_groups=mesh['dp'=8,'width'=4,'heads'=4] {'heads'}, dimensions={0} | all-to-all | bytes 2621440 | tf_op jit(solution)/shard_map/all_to_all | solution.py:17
  228.5 19.6 %all_to_all.81 = bf16[4,512,320]{1,2,0:T(8,128)(2,1)S(1)} all-to-all(bf16[4,512,320]{1,2,0:T(8,128)(2,1)S(1)} %bitcast.102), channel_id=1, replica_groups=mesh['dp'=8,'width'=4,'heads'=4] {'heads'}, dimensions={0} | all-to-all | bytes 2621440 | tf_op jit(solution)/shard_map/all_to_all | solution.py:38
  248.6 6.5 all_to_all.82
  255.4 20.9 %all_to_all.83 = bf16[4,512,320]{1,2,0:T(8,128)(2,1)S(1)} all-to-all(bf16[4,512,320]{1,2,0:T(8,128)(2,1)S(1)} %broadcast_in_dim.96), channel_id=1, replica_groups=mesh['dp'=8,'width'=4,'heads'=4] {'heads'}, dimensions={0} | all-to-all | bytes 2621440 | tf_op jit(solution)/shard_map/all_to_all | solution.py:17
  283.1 37.5 %reduce-scatter.9.cloned.1.call-done = f32[512,1280]{1,0:T(8,128)} async-done(((f32[2048,1280]{1,0:T(8,128)}), f32[512,1280]{1,0:T(8,128)}) %reduce-scatter.9.cloned.1.call-update) | async-done | bytes 2621456 | tf_op jit(solution)/shard_map/reduce_scatter | solution.py:91
  320.6 99.4 %reduce-scatter.7.cloned.1.call-done = f32[512,1280]{1,0:T(8,128)} async-done(((f32[2048,1280]{1,0:T(8,128)}), f32[512,1280]{1,0:T(8,128)}) %reduce-scatter.7.cloned.1.call-update) | async-done | bytes 2621456 | tf_op jit(solution)/shard_map/reduce_scatter | solution.py:91
  425.3 55.6 %all-gather.9.cloned.1.call-done = bf16[2048,1280]{1,0:T(8,128)(2,1)} async-done(((bf16[512,1280]{1,0:T(8,128)(2,1)}), bf16[2048,1280]{1,0:T(8,128)(2,1)}) %all-gather.9.cloned.1.call-update) | async-done | bytes 5242896 | tf_op jit(solution)/shard_map/all_gather | solution.py:82
  485.4 23.4 %all_to_all.84 = bf16[4,512,320]{1,2,0:T(8,128)(2,1)S(1)} all-to-all(bf16[4,512,320]{1,2,0:T(8,128)(2,1)S(1)} %bitcast.104), channel_id=1, replica_groups=mesh['dp'=8,'width'=4,'heads'=4] {'heads'}, dimensions={0} | all-to-all | bytes 2621440 | tf_op jit(solution)/shard_map/all_to_all | solution.py:38
  509.4 6.2 all_to_all.85
  516.0 20.7 %all_to_all.86 = bf16[4,512,320]{1,2,0:T(8,128)(2,1)S(1)} all-to-all(bf16[4,512,320]{1,2,0:T(8,128)(2,1)S(1)} %broadcast_in_dim.99), channel_id=1, replica_groups=mesh['dp'=8,'width'=4,'heads'=4] {'heads'}, dimensions={0} | all-to-all | bytes 2621440 | tf_op jit(solution)/shard_map/all_to_all | solution.py:17
  542.2 30.9 %reduce-scatter.11.cloned.1.call-done = f32[512,320]{0,1:T(8,128)} async-done(((f32[2048,320]{0,1:T(8,128)}), f32[512,320]{0,1:T(8,128)}) %reduce-scatter.11.cloned.1.call-update) | async-done | bytes 655376 | tf_op jit(solution)/shard_map/reduce_scatter | solution.py:91
  574.2 10.0 %fusion.16 = bf16[2048,5,64]{0,2,1:T(8,128)(2,1)} fusion(bf16[512,5,64]{0,2,1:T(8,128)(2,1)S(1)} %bitcast.111, f32[5,512,2048]{2,1,0:T(8,128)} %copy-done.2, f32[5,512]{1,0:T(8,128)S(1)} %log_add_fusion), kind=kOutput, calls=%fused_computation.38 | convolution fusion | flops 682229760 | bytes 22620160 | tf_op jit(solution)/shard_map/while/body/eval_jaxpr/hqk,qhd->khd/dot_general | solution.py:228
  591.1 13.7 %multiply_reduce_fusion = (f32[5,512]{1,0:T(8,128)S(1)}, f32[5,512,2048]{2,1,0:T(8,128)}) fusion(f32[5,512,2048]{2,1,0:T(8,128)} %copy-done.2, f32[5,512]{1,0:T(8,128)S(1)} %log_add_fusion, bf16[512,5,64]{0,2,1:T(8,128)(2,1)S(1)} %bitcast.112, bf16[2048,5,64]{0,2,1:T(8,128)(2,1)S(1)} %bitcast.99), kind=kOutput, calls=%fused_computation.1 | convolution fusion | flops 686814720 | bytes 43601920 | tf_op jit(solution)/shard_map/while/body/eval_jaxpr/qhd,khd->hqk/dot_general | solution.py:215
  604.8 14.6 %multiply_convert_fusion = bf16[5,512,2048]{2,1,0:T(8,128)(2,1)S(1)} fusion(f32[5,512,2048]{2,1,0:T(8,128)} %get-tuple-element.109, f32[5,512,2048]{2,1,0:T(8,128)} %copy-done.2, f32[5,512]{1,0:T(8,128)S(1)} %get-tuple-element.108, f32[5,512]{1,0:T(8,128)S(1)} %log_add_fusion), kind=kLoop, calls=%fused_computation | loop fusion | flops 20971520 | bytes 52449280 | tf_op jit(solution)/shard_map/while/body/eval_jaxpr/convert_element_type | solution.py:219
  638.7 7.3 fusion.21
  645.9 23.9 %all-to-all-done.11 = bf16[4,512,640]{1,2,0:T(8,128)(2,1)} async-done(((bf16[4,512,640]{1,2,0:T(8,128)(2,1)}), bf16[4,512,640]{1,2,0:T(8,128)(2,1)}, u32[]{:S(2)}, u32[]{:S(2)}) %all-to-all-start.11) | async-done | bytes 2621472 | tf_op jit(solution)/shard_map/all_to_all | solution.py:38
  703.8 16.3 %all-gather.11.cloned.1.call-done = bf16[2048,960]{0,1:T(8,128)(2,1)} async-done(((bf16[512,960]{0,1:T(8,128)(2,1)}), bf16[2048,960]{0,1:T(8,128)(2,1)}) %all-gather.11.cloned.1.call-update) | async-done | bytes 3932176 | tf_op jit(solution)/shard_map/all_gather | solution.py:82
  745.0 24.2 %all-reduce = (bf16[2,320]{1,0:T(2,128)(2,1)S(1)}, bf16[320]{0:T(512)(128)(2,1)S(1)}, bf16[1280]{0:T(1024)(128)(2,1)S(1)}, bf16[320]{0:T(512)(128)(2,1)S(1)}) all-reduce(bf16[2,320]{1,0:T(2,128)(2,1)S(1)} %pad_maximum_fusion.13, bf16[320]{0:T(512)(128)(2,1)S(1)} %reduce_sum.288, ...), channel_id=1, replica_groups=mesh['dp'=8,'width'=4,'heads'=4] {'dp'}, use_global_device_ids=true, to_apply=%region_31.32 | all-reduce | flops 2560 | bytes 10240 | tf_op jit(solution)/shard_map/psum | solution.py:299
  790.5 7.7 all-to-all-done.14
  799.6 33.1 %all-reduce.4.cloned.1.call-done = (bf16[3,320,320]{2,1,0:T(8,128)(2,1)}, bf16[320,320]{1,0:T(8,128)(2,1)}, bf16[320,1280]{1,0:T(8,128)(2,1)}, bf16[1280,320]{0,1:T(8,128)(2,1)}) async-done(((bf16[3,320,320]{2,1,0:T(8,128)(2,1)}, bf16[320,320]{1,0:T(8,128)(2,1)}, bf16[320,1280]{1,0:T(8,128)(2,1)}, bf16[1280,320]{0,1:T(8,128)(2,1)}), (bf16[3,320,320]{2,1,0:T(8,128)(2,1)}, bf16[320,320]{1,0:T(8,128)(2,1)}, ...) | async-done | bytes 2457616 | tf_op jit(solution)/shard_map/psum | solution.py:298
  (239 shorter events, 208.1 us)
Async XLA Ops:
  7.2 270.4 %copy-start = (bf16[320,1280]{1,0:T(8,128)(2,1)S(1)}, bf16[320,1280]{1,0:T(8,128)(2,1)}, u32[]{:S(2)}) copy-start(bf16[320,1280]{1,0:T(8,128)(2,1)} %param.19) | copy-start | bytes 2457604
  9.0 7.1 all-to-all-start
  18.4 23.2 %all-to-all-start.1 = ((bf16[4,512,320]{1,2,0:T(8,128)(2,1)}), bf16[4,512,320]{1,2,0:T(8,128)(2,1)S(1)}, u32[]{:S(2)}, u32[]{:S(2)}) async-start(bf16[4,512,320]{1,2,0:T(8,128)(2,1)} %broadcast_in_dim.91), calls=%async_computation.1 | async-start | bytes 2621440 | tf_op jit(solution)/shard_map/all_to_all | solution.py:17
  23.8 98.4 %reduce-scatter.5.cloned.1.call-start = ((), (), s32[]{:S(2)}) async-start(), calls=%async_computation.19 | async-start | bytes 9830400 | tf_op jit(solution)/shard_map/reduce_scatter | solution.py:91
  127.3 35.9 %all-to-all-start.2 = ((bf16[4,512,640]{1,2,0:T(8,128)(2,1)}), bf16[4,512,640]{1,2,0:T(8,128)(2,1)}, u32[]{:S(2)}, u32[]{:S(2)}) async-start(bf16[4,512,640]{1,2,0:T(8,128)(2,1)} %broadcast_in_dim.92), calls=%async_computation.3 | async-start | bytes 5242880 | tf_op jit(solution)/shard_map/all_to_all | solution.py:17
  131.9 93.5 %all-gather.5.cloned.1.call-start = ((), (), s32[]{:S(2)}) async-start(), calls=%async_computation.20 | async-start | bytes 1638400 | tf_op jit(solution)/shard_map/all_gather | solution.py:82
  194.2 126.4 %reduce-scatter.9.cloned.1.call-start = ((), (), s32[]{:S(2)}) async-start(), calls=%async_computation.23 | async-start | bytes 13107200 | tf_op jit(solution)/shard_map/reduce_scatter | solution.py:91
  225.3 194.7 %reduce-scatter.7.cloned.1.call-start = ((), (), s32[]{:S(2)}) async-start(), calls=%async_computation.21 | async-start | bytes 13107200 | tf_op jit(solution)/shard_map/reduce_scatter | solution.py:91
  283.1 136.9 %copy-start.44 = (f32[1280]{0:T(1024)S(1)}, f32[1280]{0:T(1024)}, u32[]{:S(2)}) copy-start(f32[1280]{0:T(1024)} %param.20) | copy-start | bytes 15364
  283.1 197.8 %all-gather.9.cloned.1.call-start = ((), (), s32[]{:S(2)}) async-start(), calls=%async_computation.24 | async-start | bytes 6553600 | tf_op jit(solution)/shard_map/all_gather | solution.py:82
  425.2 147.8 %reduce-scatter.11.cloned.1.call-start = ((), (), s32[]{:S(2)}) async-start(), calls=%async_computation.25 | async-start | bytes 3276800 | tf_op jit(solution)/shard_map/reduce_scatter | solution.py:91
  541.4 139.8 %all-gather.7.cloned.1.call-start = ((), (), s32[]{:S(2)}) async-start(), calls=%async_computation.22 | async-start | bytes 6553600 | tf_op jit(solution)/shard_map/all_gather | solution.py:82
  633.9 36.0 %all-to-all-start.11 = ((bf16[4,512,640]{1,2,0:T(8,128)(2,1)}), bf16[4,512,640]{1,2,0:T(8,128)(2,1)}, u32[]{:S(2)}, u32[]{:S(2)}) async-start(bf16[4,512,640]{1,2,0:T(8,128)(2,1)} %pad_maximum_fusion), calls=%async_computation.15 | async-start | bytes 5242880 | tf_op jit(solution)/shard_map/all_to_all | solution.py:38
  638.4 81.7 %all-gather.11.cloned.1.call-start = ((), (), s32[]{:S(2)}) async-start(), calls=%async_computation.26 | async-start | bytes 4915200 | tf_op jit(solution)/shard_map/all_gather | solution.py:82
  686.9 38.0 %all-to-all-start.6 = ((bf16[4,512,320]{1,2,0:T(8,128)(2,1)}), bf16[4,512,320]{1,2,0:T(8,128)(2,1)}, u32[]{:S(2)}, u32[]{:S(2)}) async-start(bf16[4,512,320]{1,2,0:T(8,128)(2,1)} %bitcast.101), calls=%async_computation.8 | async-start | bytes 2621440 | tf_op jit(solution)/shard_map/all_to_all | solution.py:38
  725.0 46.6 %all-to-all-start.12 = ((bf16[4,512,320]{1,2,0:T(8,128)(2,1)}), bf16[4,512,320]{1,2,0:T(8,128)(2,1)}, u32[]{:S(2)}, u32[]{:S(2)}) async-start(bf16[4,512,320]{1,2,0:T(8,128)(2,1)} %bitcast.84), calls=%async_computation.16 | async-start | bytes 2621440 | tf_op jit(solution)/shard_map/all_to_all | solution.py:38
  729.4 103.3 %all-reduce.4.cloned.1.call-start = ((), (), s32[]{:S(2)}) async-start(), calls=%async_computation.27 | async-start | bytes 5242880 | tf_op jit(solution)/shard_map/psum | solution.py:298
  742.1 31.2 %copy-start.39 = (f32[320]{0:T(512)S(1)}, f32[320]{0:T(512)}, u32[]{:S(2)}) copy-start(f32[320]{0:T(512)} %copy-done.38) | copy-start | bytes 3844
  742.1 31.2 %copy-start.41 = (f32[512]{0:T(512)S(1)}, f32[512]{0:T(512)}, u32[]{:S(2)}) copy-start(f32[512]{0:T(512)} %copy-done.40) | copy-start | bytes 6148
  742.2 31.2 %copy-start.43 = (f32[512]{0:T(512)S(1)}, f32[512]{0:T(512)}, u32[]{:S(2)}) copy-start(f32[512]{0:T(512)} %copy-done.42) | copy-start | bytes 6148
  744.9 43.2 %copy-start.24 = (bf16[512,320]{0,1:T(8,128)(2,1)S(1)}, bf16[512,320]{0,1:T(8,128)(2,1)}, u32[]{:S(2)}) copy-start(bf16[512,320]{0,1:T(8,128)(2,1)} %param.23) | copy-start | bytes 983044
  744.9 43.2 %copy-start.47 = (f32[320]{0:T(512)S(1)}, f32[320]{0:T(512)}, u32[]{:S(2)}) copy-start(f32[320]{0:T(512)} %param.22) | copy-start | bytes 3844
  774.4 7.1 all-to-all-start.13
  782.2 16.0 %all-to-all-start.14 = ((f32[32,1,1280]{2,1,0:T(1,128)}), f32[32,1,1280]{2,1,0:T(1,128)S(1)}, u32[]{:S(2)}, u32[]{:S(2)}) async-start(f32[32,1,1280]{2,1,0:T(1,128)} %broadcast_in_dim.101), calls=%async_computation.18 | async-start | bytes 327680 | tf_op jit(solution)/shard_map/all_to_all | solution.py:17
  (41 other events, 389.3 us)
Sparse Core Ops, SparseCore 0:
  47.4 74.8 reduce-scatter.4
  194.3 23.5 all-gather.4
  225.4 95.1 reduce-scatter.8
  322.9 97.0 reduce-scatter.6
  425.3 55.4 all-gather.8
  541.5 31.4 reduce-scatter.10
  575.3 55.5 all-gather.6
  675.3 44.8 all-gather.10
  734.6 97.9 all-reduce.3
where the time goes:
time: 852 us; the launch traced here: 846 us
  waiting for transfers between devices  432 us (51%)
  blocking collectives  144 us (17%)
  matrix products  98.4 us (12%)
  other arithmetic  61.8 us (7%)
  local copies, waits for them, and re-layouts  58.9 us (7%)
  starting transfers between devices  37 us (4%)
  between operations  14.8 us (2%)
    reduce_scatter x4, waiting for transfers between devices, sum_width(): lax.psum_scatter(partial_term(jnp.int32(0), row_count * lax.axis_size('wi...  242 us
    all_to_all x5, blocking collectives, copy_for_each(): return lax.all_to_all(copies, axis, split_axis=0, concat_axis=0, tiled=True)  76.4 us
    all_gather x4, waiting for transfers between devices, width_rows(): return lax.all_gather(local_part, 'width', axis=0, tiled=True)  71.9 us
    all_to_all x5, waiting for transfers between devices, copy_for_each(): return lax.all_to_all(copies, axis, split_axis=0, concat_axis=0, tiled=True)  60.5 us
    all_to_all x2, blocking collectives, sum_at_owner(): lax.all_to_all(pieces, axis, split_axis=0, concat_axis=0, tiled=True)  43 us
    psum x1, waiting for transfers between devices, shards(): lax.psum(d_w_attn.astype(jnp.bfloat16), 'dp').astype(jnp.float32)  33.1 us
    psum x1, blocking collectives, shards(): lax.psum(d_b_qv.astype(jnp.bfloat16), 'dp').astype(jnp.float32)  24.2 us
    all_to_all x3, waiting for transfers between devices, sum_at_owner(): lax.all_to_all(pieces, axis, split_axis=0, concat_axis=0, tiled=True)  23.9 us
  transfers between devices with their start and end apart: 17, of which 13 were waited for; matrix products, arithmetic and copies ran while one was open for 17% of the time, Pallas kernels for 0%

commit v1 on v0

v1 whole, which is shorter than its diff:
```python
import functools
import jax
import jax.numpy as jnp
from jax import lax
from jax.experimental import pallas as pl
from jax.experimental.pallas import tpu as pltpu
from jax.sharding import PartitionSpec as P

F32, BF16 = jnp.float32, jnp.bfloat16
D, HS, ROWS, PART, QUARTER = 1280, 64, 128, 320, 512
HEADS = 5
EPSILON = 1e-05
GELU_COEF = 0.7978845608028654
MASKED = -1e30
VMEM = pl.BlockSpec(memory_space=pltpu.VMEM)


def nn(a, b):
    return jnp.dot(a, b, preferred_element_type=F32)


def nt(a, b):
    return lax.dot_general(a, b, (((1,), (1,)), ((), ())), preferred_element_type=F32)


def tn(a, b):
    return lax.dot_general(a, b, (((0,), (0,)), ((), ())), preferred_element_type=F32)


class Place:
    def __init__(self):
        self.dp, self.w, self.h = (lax.axis_index(n) for n in ("dp", "width", "heads"))
        self.wc = self.w + 1 - 2 * lax.rem(self.w, 2)
        self.wy = lax.rem(self.w + 2, 4)
        self.wyc = lax.rem(self.wc + 2, 4)
        self.core = (self.dp, self.wc, self.h)
        self.near = (self.dp, self.wy, self.h)
        self.near_core = (self.dp, self.wyc, self.h)
        self.far = (lax.rem(self.dp + 4, 8), self.wy, self.h)

    def z(self, k):
        return (self.dp, self.w, lax.rem(self.h + k, 4))


def sub_block(quarter, w):
    return w + lax.rem(quarter, 2) * (3 - 2 * w)


def greet(devices):
    barrier = pltpu.get_barrier_semaphore()
    for device in devices:
        pl.semaphore_signal(barrier, inc=1, device_id=device, device_id_type=pl.DeviceIdType.MESH)
    pl.semaphore_wait(barrier, len(devices))


class Links:
    def __init__(self, sent, landed):
        self.sent, self.landed, self.count = sent, landed, 0

    def send(self, source, target, device):
        i = self.count
        self.count += 1
        copy = pltpu.make_async_remote_copy(
            src_ref=source, dst_ref=target, send_sem=self.sent.at[i], recv_sem=self.landed.at[i],
            device_id=device, device_id_type=pl.DeviceIdType.MESH,
        )
        copy.start()
        return copy


def rows_of(start, size=ROWS):
    return pl.ds(pl.multiple_of(start, size), size)


def norm_stats(values):
    mean = jnp.mean(values, axis=1, keepdims=True)
    centred = values - mean
    scale = lax.rsqrt(jnp.mean(centred * centred, axis=1, keepdims=True) + EPSILON)
    return centred * scale, scale


def enter_kernel(
    tok, dout, gain, shift, b_proj, b_out, wa, wp, bqv,
    x_o, d_o, vec_o, x1_o, q_o, kv_o, wa_o, wp_o,
    xa, da, vl, vg, sent, landed,
):
    at = Place()
    w, h = at.w, at.h
    links = Links(sent, landed)
    vl[0:2, :] = gain[...]
    vl[2:4, :] = shift[...]
    vl[4:5, :] = b_proj[...]
    vl[5:6, :] = b_out[...]
    vl[6:8, :] = jnp.zeros((2, PART), F32)
    greet([at.core, at.near, at.near_core, at.far, at.z(1), at.z(2), at.z(3)])
    peers = [(at.near, at.wy), (at.near_core, at.wyc), (at.core, at.wc)]
    arrive_x, arrive_v, arrive_d = [], [], []
    for device, peer in peers:
        mine = tok.at[rows_of(sub_block(h, peer) * ROWS)]
        arrive_x.append(links.send(mine, xa.at[w], device))
    for device, peer in peers:
        arrive_v.append(links.send(vl, vg.at[w], device))
    block = pl.ds(pl.multiple_of(w * PART, 64), PART)
    other = pl.ds(pl.multiple_of(at.wy * PART, 64), PART)
    kv_far = links.send(wa.at[1:3], wa_o.at[1:3, block], at.far)
    kv_core = links.send(wa.at[1:3], wa_o.at[1:3, block], at.core)
    for device, peer in peers:
        mine = dout.at[rows_of(sub_block(h, peer) * ROWS)]
        arrive_d.append(links.send(mine, da.at[w], device))
    q_near = links.send(wa.at[0], wa_o.at[0, block], at.near)
    q_core = links.send(wa.at[0], wa_o.at[0, block], at.core)
    p_far = links.send(wp, wp_o.at[w], at.far)
    p_core = links.send(wp, wp_o.at[w], at.core)
    own = rows_of(sub_block(h, w) * ROWS)
    xa[w] = tok[own, :]
    da[w] = dout[own, :]
    vg[w] = vl[...]
    for i in range(3):
        wa_o[i, block, :] = wa[i]
    wp_o[w] = wp[...]
    for copy in arrive_x + arrive_v:
        copy.wait_recv()
    vec = jnp.concatenate([vg[i] for i in range(4)], axis=1)
    vec_o[...] = vec
    x = jnp.concatenate([xa[i] for i in range(4)], axis=1)
    x_o[...] = x
    unit, _ = norm_stats(x.astype(F32))
    x1_o[rows_of(h * ROWS), :] = (unit * vec[0:1] + vec[2:3]).astype(BF16)
    mine = x1_o.at[rows_of(h * ROWS)]
    gather = {k: links.send(mine, mine, at.z(k)) for k in (1, 3, 2)}
    kv_far.wait_recv()
    forwards = [links.send(wa_o.at[1:3, other], wa_o.at[1:3, other], at.core)]
    kv_core.wait_recv()
    forwards[0].wait_recv()
    shares, passed = [], []

    def key_block(c, who):
        return kv_o.at[rows_of((c * 4 + sub_block(c, who)) * ROWS)]

    chunks = [lax.rem(h + i, 4) for i in (0, 1, 3, 2)]
    for i, c in enumerate(chunks):
        if i:
            gather[4 - (0, 1, 3, 2)[i]].wait_recv()
        rows = x1_o[rows_of(c * ROWS), :]
        keys = nn(rows, wa_o[1]).astype(BF16)
        values = (nn(rows, wa_o[2]) + bqv[1:2]).astype(BF16)
        pieces = []
        for head in range(HEADS):
            part = slice(head * HS, (head + 1) * HS)
            pieces += [keys[:, part], values[:, part]]
        key_block(c, w)[...] = jnp.concatenate(pieces, axis=1)
        shares.append(links.send(key_block(c, w), key_block(c, w), at.near))
        shares.append(links.send(key_block(c, w), key_block(c, w), at.core))
    q_near.wait_recv()
    forwards.append(links.send(wa_o.at[0, other], wa_o.at[0, other], at.core))
    p_far.wait_recv()
    forwards.append(links.send(wp_o.at[at.wy], wp_o.at[at.wy], at.core))
    for i, c in enumerate(chunks):
        shares[2 * i].wait_recv()
        passed.append(links.send(key_block(c, at.wy), key_block(c, at.wy), at.core))
    q_core.wait_recv()
    forwards[1].wait_recv()
    zeros = jnp.zeros((ROWS, HS), BF16)
    for c in range(4):
        rows = x1_o[c * ROWS : (c + 1) * ROWS, :]
        queries = ((nn(rows, wa_o[0]) + bqv[0:1]).astype(BF16).astype(F32) * HS**-0.5).astype(BF16)
        pieces = []
        for head in range(HEADS):
            pieces += [queries[:, head * HS : (head + 1) * HS], zeros]
        q_o[c * ROWS : (c + 1) * ROWS, :] = jnp.concatenate(pieces, axis=1)
    for copy in arrive_d:
        copy.wait_recv()
    d_o[...] = jnp.concatenate([da[i] for i in range(4)], axis=1)
    p_core.wait_recv()
    forwards[2].wait_recv()
    for i in range(4):
        shares[2 * i + 1].wait_recv()
        passed[i].wait_recv()
    for copy in arrive_x + arrive_v + arrive_d + [kv_far, kv_core, q_near, q_core, p_far, p_core]:
        copy.wait_send()
    for copy in list(gather.values()) + forwards + shares + passed:
        copy.wait_send()


def enter(tok, dout, gain, shift, b_proj, b_out, wa, wp, bqv):
    return pl.pallas_call(
        enter_kernel,
        name="enter",
        out_shape=(
            jax.ShapeDtypeStruct((ROWS, D), BF16),
            jax.ShapeDtypeStruct((ROWS, D), BF16),
            jax.ShapeDtypeStruct((8, D), F32),
            jax.ShapeDtypeStruct((QUARTER, D), BF16),
            jax.ShapeDtypeStruct((QUARTER, 640), BF16),
            jax.ShapeDtypeStruct((2048, 640), BF16),
            jax.ShapeDtypeStruct((3, D, PART), BF16),
            jax.ShapeDtypeStruct((4, PART, PART), BF16),
        ),
        in_specs=[VMEM] * 9,
        out_specs=(VMEM,) * 8,
        scratch_shapes=[
            pltpu.VMEM((4, ROWS, PART), BF16),
            pltpu.VMEM((4, ROWS, PART), BF16),
            pltpu.VMEM((8, PART), F32),
            pltpu.VMEM((4, 8, PART), F32),
            pltpu.SemaphoreType.DMA((48,)),
            pltpu.SemaphoreType.DMA((48,)),
        ],
        compiler_params=pltpu.CompilerParams(collective_id=1, has_side_effects=True, vmem_limit_bytes=56 * 2**20),
    )(tok, dout, gain, shift, b_proj, b_out, wa, wp, bqv)
ORDER = (1, 3, 2)


def visible_scores(scores, quarter, shift):
    last = scores[quarter * QUARTER :]
    key = lax.broadcasted_iota(jnp.int32, last.shape, 0)
    query = lax.broadcasted_iota(jnp.int32, last.shape, 1) + shift
    last = jnp.where(key <= query, last, MASKED)
    return last if quarter == 0 else jnp.concatenate([scores[: quarter * QUARTER], last], axis=0)


def attend_kernel(
    q, kv, wp, x, d, vec, wf, wo,
    att_o, lse_o, kvt_o, middle_o, x2_o, d_all, wf_o, wo_o, wp_o,
    att_t, stage, parts, wog, sent, landed,
):
    at = Place()
    w, h = at.w, at.h
    links = Links(sent, landed)
    greet([at.core, at.near, at.far, at.z(1), at.z(2), at.z(3)])
    block = pl.ds(pl.multiple_of(w * PART, 64), PART)
    other = pl.ds(pl.multiple_of(at.wy * PART, 64), PART)
    own = rows_of(h * ROWS)
    f_near = links.send(wf, wf_o.at[block], at.near)
    o_far = links.send(wo, wog.at[w], at.far)
    f_core = links.send(wf, wf_o.at[block], at.core)
    o_core = links.send(wo, wog.at[w], at.core)
    d_all[own, :] = d[...]
    d_moves = [links.send(d, d_all.at[own], at.z(k)) for k in ORDER]
    wf_o[block, :] = wf[...]
    wog[w] = wo[...]
    wp_o[...] = jnp.concatenate([wp[i] for i in range(4)], axis=1)

    @pl.loop(0, HEADS)
    def _(head):
        tile = pl.ds(pl.multiple_of(head * 128, 128), 128)
        kvt_o[tile, :] = kv[:, tile].T

    base = links.count

    def attend_chunk(j):
        keys = (j + 1) * QUARTER
        shift = sub_block(j, w) * ROWS

        @pl.loop(0, HEADS)
        def _(head):
            tile = pl.ds(pl.multiple_of(head * 128, 128), 128)
            scores = nt(kv[0:keys, tile], q[j * ROWS : (j + 1) * ROWS, tile])
            scores = visible_scores(scores, j, shift)
            peak = jnp.max(scores, axis=0, keepdims=True)
            weights = jnp.exp(scores - peak)
            total = jnp.sum(weights, axis=0, keepdims=True)
            probs = (weights * (1.0 / total)).astype(BF16)
            result = nn(kvt_o[tile, 0:keys], probs)
            att_t[pl.ds(pl.multiple_of(head * HS, HS), HS), :] = result[HS:, :]
            lse_o[pl.ds(j * 8 + head, 1), :] = peak + jnp.log(total)

    def move(i, j):
        return pltpu.make_async_remote_copy(
            src_ref=stage.at[j], dst_ref=parts.at[i], send_sem=sent.at[base + i], recv_sem=landed.at[base + i],
            device_id=(at.dp, w, j), device_id_type=pl.DeviceIdType.MESH,
        )

    @pl.loop(0, 4)
    def _(i):
        j = lax.rem(h + i + 1, 4)
        for case in range(4):
            pl.when(j == case)(functools.partial(attend_chunk, case))
        attended = att_t[...].T.astype(BF16)
        att_o[rows_of(j * ROWS), :] = attended
        stage[j] = nn(attended, wp_o[...]).astype(BF16)

        @pl.when(i < 3)
        def _():
            move(i, j).start()

    links.count += 3
    f_near.wait_recv()
    f_pass = links.send(wf_o.at[other], wf_o.at[other], at.core)
    o_far.wait_recv()
    o_pass = links.send(wog.at[at.wy], wog.at[at.wy], at.core)
    middle = x[...].astype(F32) + vec[4:5, :] + stage[h].astype(F32)
    for i in range(3):
        move(i, lax.rem(h + i + 1, 4)).wait()
        middle = middle + parts[i].astype(F32)
    middle_o[...] = middle
    unit, _ = norm_stats(middle)
    x2_o[...] = (unit * vec[1:2] + vec[3:4]).astype(BF16)
    o_core.wait_recv()
    o_pass.wait_recv()

    @pl.loop(0, 10)
    def _(i):
        rows = rows_of(i * ROWS)
        wo_o[rows, :] = jnp.concatenate([wog[part, rows, :] for part in range(4)], axis=1)

    f_core.wait_recv()
    f_pass.wait_recv()
    for copy in d_moves:
        copy.wait()
    for copy in (f_near, o_far, f_core, o_core, f_pass, o_pass):
        copy.wait_send()


def attend(q, kv, wp, x, d, vec, wf, wo):
    return pl.pallas_call(
        attend_kernel,
        name="attend",
        out_shape=(
            jax.ShapeDtypeStruct((QUARTER, PART), BF16),
            jax.ShapeDtypeStruct((32, 128), F32),
            jax.ShapeDtypeStruct((640, 2048), BF16),
            jax.ShapeDtypeStruct((ROWS, D), F32),
            jax.ShapeDtypeStruct((ROWS, D), BF16),
            jax.ShapeDtypeStruct((QUARTER, D), BF16),
            jax.ShapeDtypeStruct((D, D), BF16),
            jax.ShapeDtypeStruct((D, D), BF16),
            jax.ShapeDtypeStruct((PART, D), BF16),
        ),
        in_specs=[VMEM] * 8,
        out_specs=(VMEM,) * 9,
        scratch_shapes=[
            pltpu.VMEM((PART, ROWS), F32),
            pltpu.VMEM((4, ROWS, D), BF16),
            pltpu.VMEM((3, ROWS, D), BF16),
            pltpu.VMEM((4, D, PART), BF16),
            pltpu.SemaphoreType.DMA((16,)),
            pltpu.SemaphoreType.DMA((16,)),
        ],
        compiler_params=pltpu.CompilerParams(collective_id=2, has_side_effects=True, vmem_limit_bytes=56 * 2**20),
    )(q, kv, wp, x, d, vec, wf, wo)


def norm_gradient(grad, unit, scale, gain):
    scaled = grad * gain
    mean = jnp.mean(scaled, axis=1, keepdims=True)
    along = jnp.mean(scaled * unit, axis=1, keepdims=True)
    return scale * (scaled - mean - unit * along)


def feed_kernel(
    x2, middle, d_all, wf, wo, b_fc, vec,
    out_o, gm_o, gb_o, dwf_o, dwo_o, sums_o, dbf_o,
    x2_all, gh, hid, gp, stage, parts, stage_b, parts_b, back, sent, landed,
):
    at = Place()
    w, h = at.w, at.h
    links = Links(sent, landed)
    greet([at.core, at.near, at.near_core, at.z(1), at.z(2), at.z(3)])
    own = rows_of(h * ROWS)
    x2_all[own, :] = x2[...]
    gather = {k: links.send(x2, x2_all.at[own], at.z(k)) for k in ORDER}
    tiles = D // 256

    @pl.loop(0, tiles)
    def _(i):
        tile = pl.ds(pl.multiple_of(i * 256, 256), 256)
        gh[:, tile] = nt(d_all[...], wo[tile, :])

    chunks = [lax.rem(h + i, 4) for i in (0, 1, 3, 2)]
    moves = []
    for i, c in enumerate(chunks):
        k = (0, 1, 3, 2)[i]
        if i:
            gather[4 - k].wait_recv()
        rows = rows_of(c * ROWS)

        @pl.loop(0, tiles)
        def _(t):
            tile = pl.ds(pl.multiple_of(t * 256, 256), 256)
            u = nn(x2_all[rows, :], wf[:, tile]) + b_fc[:, tile]
            square = u * u
            th = jnp.tanh(GELU_COEF * (u + 0.044715 * square * u))
            hid[rows, tile] = (0.5 * u * (1.0 + th)).astype(BF16)
            slope = 0.5 * (1.0 + th) + 0.5 * u * (1.0 - th * th) * (GELU_COEF * (1.0 + 0.134145 * square))
            gp[rows, tile] = (gh[rows, tile] * slope).astype(BF16)

        @pl.loop(0, tiles)
        def _(t):
            tile = pl.ds(pl.multiple_of(t * 256, 256), 256)
            stage[c, :, tile] = nt(gp[rows, :], wf[tile, :]).astype(BF16)

        if i:
            moves.append(links.send(stage.at[c], parts.at[i - 1], at.z(k)))

    @pl.loop(0, tiles)
    def _(t):
        tile = pl.ds(pl.multiple_of(t * 256, 256), 256)
        stage_b[:, tile] = nn(hid[...], wo[:, tile]).astype(BF16)

    moves_b = [
        links.send(stage_b.at[rows_of(chunks[i] * ROWS)], parts_b.at[i - 1], at.z((0, 1, 3, 2)[i])) for i in (1, 2, 3)
    ]
    dbf_o[...] = jnp.sum(gp[...].astype(F32), axis=0, keepdims=True)

    @pl.loop(0, tiles)
    def _(t):
        tile = pl.ds(pl.multiple_of(t * 256, 256), 256)
        dwf_o[tile, :] = tn(x2_all[:, tile], gp[...]).astype(BF16)
        dwo_o[tile, :] = tn(hid[:, tile], d_all[...]).astype(BF16)

    grad_normed = stage[h].astype(F32)
    for i in range(3):
        moves[i].wait_recv()
        grad_normed = grad_normed + parts[i].astype(F32)
    unit, scale = norm_stats(middle[...])
    grad = d_all[own, :].astype(F32)
    grad_middle = grad + norm_gradient(grad_normed, unit, scale, vec[1:2, :])
    gm_o[...] = grad_middle
    branch = grad_middle.astype(BF16)
    gb_o[...] = branch
    sums_o[0:1, :] = jnp.sum(grad_normed * unit, axis=0, keepdims=True)
    sums_o[1:2, :] = jnp.sum(grad_normed, axis=0, keepdims=True)
    sums_o[2:3, :] = jnp.sum(grad, axis=0, keepdims=True)
    sums_o[3:4, :] = jnp.sum(branch.astype(F32), axis=0, keepdims=True)
    sums_o[4:8, :] = jnp.zeros((4, D), F32)
    result = middle[...] + vec[5:6, :] + stage_b[own, :].astype(F32)
    for i in range(3):
        moves_b[i].wait_recv()
        result = result + parts_b[i].astype(F32)
    result = result.astype(BF16)
    for part in range(4):
        back[part] = result[:, part * PART : (part + 1) * PART]
    mine = sub_block(h, w)
    out_o[mine] = back[w]
    returns = [
        links.send(back.at[peer], out_o.at[mine], device)
        for device, peer in ((at.near, at.wy), (at.near_core, at.wyc), (at.core, at.wc))
    ]
    for copy in returns:
        copy.wait_recv()
    for copy in list(gather.values()) + moves + moves_b + returns:
        copy.wait_send()


def feed(x2, middle, d_all, wf, wo, b_fc, vec):
    return pl.pallas_call(
        feed_kernel,
        name="feed",
        out_shape=(
            jax.ShapeDtypeStruct((4, ROWS, PART), BF16),
            jax.ShapeDtypeStruct((ROWS, D), F32),
            jax.ShapeDtypeStruct((ROWS, D), BF16),
            jax.ShapeDtypeStruct((D, D), BF16),
            jax.ShapeDtypeStruct((D, D), BF16),
            jax.ShapeDtypeStruct((8, D), F32),
            jax.ShapeDtypeStruct((1, D), F32),
        ),
        in_specs=[VMEM] * 7,
        out_specs=(VMEM,) * 7,
        scratch_shapes=[
            pltpu.VMEM((QUARTER, D), BF16),
            pltpu.VMEM((QUARTER, D), F32),
            pltpu.VMEM((QUARTER, D), BF16),
            pltpu.VMEM((QUARTER, D), BF16),
            pltpu.VMEM((4, ROWS, D), BF16),
            pltpu.VMEM((3, ROWS, D), BF16),
            pltpu.VMEM((QUARTER, D), BF16),
            pltpu.VMEM((3, ROWS, D), BF16),
            pltpu.VMEM((4, ROWS, PART), BF16),
            pltpu.SemaphoreType.DMA((16,)),
            pltpu.SemaphoreType.DMA((16,)),
        ],
        compiler_params=pltpu.CompilerParams(collective_id=3, has_side_effects=True, vmem_limit_bytes=56 * 2**20),
    )(x2, middle, d_all, wf, wo, b_fc, vec)


def attend_back_kernel(
    gb, att, lse, q, kv, kvt, wp,
    gmx_o, dwp_o,
    g_all, go, dq_t, dkv, give, take, give_y, take_y, sent, landed,
):
    at = Place()
    w, h = at.w, at.h
    links = Links(sent, landed)
    greet([at.core, at.near, at.z(1), at.z(2), at.z(3)])
    own = rows_of(h * ROWS)
    g_all[own, :] = gb[...]
    gather = {k: links.send(gb, g_all.at[own], at.z(k)) for k in ORDER}
    dkv[...] = jnp.zeros(dkv.shape, F32)
    zeros = jnp.zeros((ROWS, HS), BF16)

    def back_chunk(j):
        keys = (j + 1) * QUARTER
        shift = sub_block(j, w) * ROWS
        rows = slice(j * ROWS, (j + 1) * ROWS)

        @pl.loop(0, HEADS)
        def _(head):
            tile = pl.ds(pl.multiple_of(head * 128, 128), 128)
            query, grad = q[rows, tile], go[:, tile]
            scores = visible_scores(nt(kv[0:keys, tile], query), j, shift)
            probs = jnp.exp(scores - lse[pl.ds(j * 8 + head, 1), :])
            grad_probs = nt(kv[0:keys, tile], grad)
            inner = jnp.sum(grad_probs * probs, axis=0, keepdims=True)
            grad_scores = (probs * (grad_probs - inner)).astype(BF16)
            both = jnp.concatenate([grad_scores, probs.astype(BF16)], axis=1)
            dkv[0:keys, tile] += nn(both, jnp.concatenate([query, grad], axis=0))
            result = nn(kvt[tile, 0:keys], grad_scores)
            dq_t[pl.ds(pl.multiple_of(head * HS, HS), HS), :] = result[:HS, :] * HS**-0.5

    for i in range(4):
        k = (0, 1, 3, 2)[i]
        if i:
            gather[4 - k].wait_recv()
        c = lax.rem(h + k, 4)
        rows = rows_of(c * ROWS)
        grad = nt(g_all[rows, :], wp[...]).astype(BF16)
        pieces = []
        for head in range(HEADS):
            pieces += [zeros, grad[:, head * HS : (head + 1) * HS]]
        go[...] = jnp.concatenate(pieces, axis=1)
        for case in range(4):
            pl.when(c == case)(functools.partial(back_chunk, case))
        gmx_o[rows, 0:PART] = dq_t[...].T.astype(BF16)

    def piece(who, j):
        return dkv[rows_of((j * 4 + sub_block(j, who)) * ROWS), :]

    for j in range(4):
        rows = slice(j * ROWS, (j + 1) * ROWS)
        give[1, rows, :] = piece(at.wyc, j).astype(BF16)
    moves = [links.send(give.at[1], take.at[1], at.core)]
    for j in range(4):
        rows = slice(j * ROWS, (j + 1) * ROWS)
        give[0, rows, :] = piece(at.wc, j).astype(BF16)
    moves.append(links.send(give.at[0], take.at[0], at.core))
    moves[0].wait_recv()
    for j in range(4):
        rows = slice(j * ROWS, (j + 1) * ROWS)
        give_y[rows, :] = (piece(at.wy, j) + take[1, rows, :].astype(F32)).astype(BF16)
    moves.append(links.send(give_y, take_y, at.near))
    for i in range(4):
        part = slice(i * PART, (i + 1) * PART)
        dwp_o[i] = tn(att[...], g_all[:, part]).astype(BF16)
    moves[1].wait_recv()
    moves[2].wait_recv()
    for j in range(4):
        rows = slice(j * ROWS, (j + 1) * ROWS)
        total = (piece(w, j) + take[0, rows, :].astype(F32) + take_y[rows, :].astype(F32)).astype(BF16)
        pieces = [total[:, head * 128 : head * 128 + HS] for head in range(HEADS)]
        pieces += [total[:, head * 128 + HS : (head + 1) * 128] for head in range(HEADS)]
        gmx_o[rows, PART:] = jnp.concatenate(pieces, axis=1)
    for copy in list(gather.values()) + moves:
        copy.wait_send()


def attend_back(gb, att, lse, q, kv, kvt, wp):
    return pl.pallas_call(
        attend_back_kernel,
        name="attend_back",
        out_shape=(
            jax.ShapeDtypeStruct((QUARTER, 3 * PART), BF16),
            jax.ShapeDtypeStruct((4, PART, PART), BF16),
        ),
        in_specs=[VMEM] * 7,
        out_specs=(VMEM,) * 2,
        scratch_shapes=[
            pltpu.VMEM((QUARTER, D), BF16),
            pltpu.VMEM((ROWS, 640), BF16),
            pltpu.VMEM((PART, ROWS), F32),
            pltpu.VMEM((2048, 640), F32),
            pltpu.VMEM((2, QUARTER, 640), BF16),
            pltpu.VMEM((2, QUARTER, 640), BF16),
            pltpu.VMEM((QUARTER, 640), BF16),
            pltpu.VMEM((QUARTER, 640), BF16),
            pltpu.SemaphoreType.DMA((8,)),
            pltpu.SemaphoreType.DMA((8,)),
        ],
        compiler_params=pltpu.CompilerParams(collective_id=4, has_side_effects=True, vmem_limit_bytes=56 * 2**20),
    )(gb, att, lse, q, kv, kvt, wp)


def leave_kernel(
    gmx, wa, x1, x, gm, vec,
    dt_o, dwa_o, dbqv_o, sums_o,
    stage, parts, back, sent, landed,
):
    at = Place()
    w, h = at.w, at.h
    links = Links(sent, landed)
    greet([at.core, at.near, at.near_core, at.z(1), at.z(2), at.z(3)])
    moves = []
    for k in (2, 1, 3, 0):
        c = lax.rem(h + k, 4)
        rows = rows_of(c * ROWS)
        partial = nt(gmx[rows, 0:PART], wa[0])
        for i in (1, 2):
            partial = partial + nt(gmx[rows, i * PART : (i + 1) * PART], wa[i])
        stage[c] = partial.astype(BF16)
        if k:
            moves.append(links.send(stage.at[c], parts.at[k - 1], at.z(k)))

    @pl.loop(0, D // 256)
    def _(t):
        tile = pl.ds(pl.multiple_of(t * 256, 256), 256)
        dwa_o[tile, :] = tn(x1[:, tile], gmx[...]).astype(BF16)

    mixed = jnp.sum(gmx[...].astype(F32), axis=0, keepdims=True)
    dbqv_o[0:1, :] = mixed[:, :PART]
    dbqv_o[1:2, :] = mixed[:, 2 * PART :]
    grad_normed = stage[h].astype(F32)
    for copy, k in zip(moves, (2, 1, 3)):
        copy.wait_recv()
        grad_normed = grad_normed + parts[k - 1].astype(F32)
    unit, scale = norm_stats(x[...].astype(F32))
    result = (gm[...] + norm_gradient(grad_normed, unit, scale, vec[0:1, :])).astype(BF16)
    sums_o[0:1, :] = jnp.sum(grad_normed * unit, axis=0, keepdims=True)
    sums_o[1:2, :] = jnp.sum(grad_normed, axis=0, keepdims=True)
    sums_o[2:8, :] = jnp.zeros((6, D), F32)
    for part in range(4):
        back[part] = result[:, part * PART : (part + 1) * PART]
    mine = sub_block(h, w)
    dt_o[mine] = back[w]
    returns = [
        links.send(back.at[peer], dt_o.at[mine], device)
        for device, peer in ((at.near, at.wy), (at.near_core, at.wyc), (at.core, at.wc))
    ]
    for copy in returns:
        copy.wait_recv()
    for copy in moves + returns:
        copy.wait_send()


def leave(gmx, wa, x1, x, gm, vec):
    return pl.pallas_call(
        leave_kernel,
        name="leave",
        out_shape=(
            jax.ShapeDtypeStruct((4, ROWS, PART), BF16),
            jax.ShapeDtypeStruct((D, 3 * PART), BF16),
            jax.ShapeDtypeStruct((2, PART), F32),
            jax.ShapeDtypeStruct((8, D), F32),
        ),
        in_specs=[VMEM] * 6,
        out_specs=(VMEM,) * 4,
        scratch_shapes=[
            pltpu.VMEM((4, ROWS, D), BF16),
            pltpu.VMEM((3, ROWS, D), BF16),
            pltpu.VMEM((4, ROWS, PART), BF16),
            pltpu.SemaphoreType.DMA((8,)),
            pltpu.SemaphoreType.DMA((8,)),
        ],
        compiler_params=pltpu.CompilerParams(collective_id=5, has_side_effects=True, vmem_limit_bytes=56 * 2**20),
    )(gmx, wa, x1, x, gm, vec)


def shards(tokens, ln_gain, ln_bias, w_attn, b_qv, w_proj, b_proj, w_fc, b_fc, w_out, b_out, d_out):
    x, d, vec, x1, q, kv, wa, wp = enter(
        tokens, d_out, ln_gain, ln_bias, b_proj.reshape(1, -1), b_out.reshape(1, -1), w_attn, w_proj, b_qv
    )
    att, lse, kvt, middle, x2, d_all, wf, wo, wp = attend(q, kv, wp, x, d, vec, w_fc, w_out)
    block_out, gm, gb, dwf, dwo, sums_second, dbf = feed(x2, middle, d_all, wf, wo, b_fc.reshape(1, -1), vec)
    gmx, dwp = attend_back(gb, att, lse, q, kv, kvt, wp)
    d_tokens, dwa, dbqv, sums_first = leave(gmx, wa, x1, x, gm, vec)

    def scatter(grad, dim):
        return lax.psum_scatter(grad, "width", scatter_dimension=dim, tiled=True)

    d_w_fc = lax.psum(scatter(dwf, 0), "dp").astype(F32)
    d_w_out = lax.psum(scatter(dwo, 1), "dp").astype(F32)
    d_w_proj = lax.psum(scatter(dwp, 0), "dp").astype(F32)[0]
    d_w_attn = lax.psum(scatter(dwa, 0), "dp").astype(F32).reshape(PART, 3, PART).transpose(1, 0, 2)
    sums = lax.psum(jnp.concatenate([sums_first[0:2], sums_second[0:4]], 0), ("dp", "heads", "width"))
    sums = lax.dynamic_slice_in_dim(sums, lax.axis_index("width") * PART, PART, 1)
    d_ln_gain = jnp.stack((sums[0], sums[2]))
    d_ln_bias = jnp.stack((sums[1], sums[3]))
    d_b_out, d_b_proj = sums[4], sums[5]
    d_b_fc, d_b_qv = lax.psum((dbf, dbqv), ("dp", "width"))
    return (
        block_out.reshape(QUARTER, PART),
        d_tokens.reshape(QUARTER, PART),
        d_ln_gain,
        d_ln_bias,
        d_w_attn,
        d_b_qv,
        d_w_proj,
        d_b_proj,
        d_w_fc,
        d_b_fc[0],
        d_w_out,
        d_b_out,
    )
def solution(mesh):
    in_specs = (
        P(("dp", "heads"), "width"),
        P(None, "width"),
        P(None, "width"),
        P(None, "width", "heads"),
        P(None, "heads"),
        P("heads", "width"),
        P("width"),
        P("width", "heads"),
        P("heads"),
        P("heads", "width"),
        P("width"),
        P(("dp", "heads"), "width"),
    )
    out_specs = (
        P(("dp", "heads"), "width"),
        P(("dp", "heads"), "width"),
        P(None, "width"),
        P(None, "width"),
        P(None, "width", "heads"),
        P(None, "heads"),
        P("heads", "width"),
        P("width"),
        P("width", "heads"),
        P("heads"),
        P("heads", "width"),
        P("width"),
    )
    return jax.shard_map(shards, mesh=mesh, in_specs=in_specs, out_specs=out_specs, check_vma=False)
```

time: 852 us -> 611 us (0.72)
  waiting for transfers between devices: 432 us -> 130 us
  Pallas kernels: 0 us -> 241 us
  matrix products: 98.4 us -> 0 us
  other arithmetic: 61.8 us -> 3.98 us
  blocking collectives: 144 us -> 194 us
  starting transfers between devices: 37 us -> 0.2 us
  local copies, waits for them, and re-layouts: 58.9 us -> 23.1 us
    pallas_call x0 -> x5, Pallas kernels: none -> 241 us  [the longest x1 60.5 us: attend_back(): pl.pallas_call(attend_back_kernel, name='attend_back', out_shape=(jax.Sha...]
    psum x1 -> x2, blocking collectives: 24.2 us -> 194 us  [the longest x1 131 us: shards(): d_b_fc, d_b_qv = lax.psum((dbf, dbqv), ('dp', 'width'))]
    reduce_scatter x4 -> x3, waiting for transfers between devices: 242 us -> 89.4 us  [scatter(): return lax.psum_scatter(grad, 'width', scatter_dimension=dim, tiled=True)]
    all_to_all x7 -> x0, blocking collectives: 119 us -> none  [the longest x5 76.4 us: copy_for_each(): return lax.all_to_all(copies, axis, split_axis=0, concat_axis=0, tiled=True)]
    dot_general x18 -> x0, matrix products: 98.4 us -> none  [the longest x4 17.6 us: dot_rows(): return jnp.dot(left_side, right_side, preferred_element_type=jnp.float32)]
    all_to_all x8 -> x0, waiting for transfers between devices: 84.4 us -> none  [the longest x5 60.5 us: copy_for_each(): return lax.all_to_all(copies, axis, split_axis=0, concat_axis=0, tiled=True)]
    all_gather x4 -> x0, waiting for transfers between devices: 71.9 us -> none  [width_rows(): return lax.all_gather(local_part, 'width', axis=0, tiled=True)]
    unnamed x9 -> x6, waiting for transfers between devices: 0.36 us -> 40.3 us
  transfers between devices with their start and end apart: 17 -> 5, of which waited for: 13 -> 4; matrix products, arithmetic and copies ran while one was open for 17% -> 2% of each run, Pallas kernels for 0% -> 0%
where the time goes in v1:
time: 611 us; the launch traced here: 606 us
  Pallas kernels  241 us (39%)
  blocking collectives  194 us (32%)
  waiting for transfers between devices  130 us (21%)
  local copies, waits for them, and re-layouts  23.1 us (4%)
  between operations  14.1 us (2%)
    psum x1, blocking collectives, shards(): d_b_fc, d_b_qv = lax.psum((dbf, dbqv), ('dp', 'width'))  131 us
    reduce_scatter x3, waiting for transfers between devices, scatter(): return lax.psum_scatter(grad, 'width', scatter_dimension=dim, tiled=True)  89.4 us
    psum x1, blocking collectives, shards(): lax.psum(jnp.concatenate([sums_first[0:2], sums_second[0:4]], 0), ('dp',...  63 us
    pallas_call x1, Pallas kernels, attend_back(): pl.pallas_call(attend_back_kernel, name='attend_back', out_shape=(jax.Sha...  60.5 us
    pallas_call x1, Pallas kernels, feed(): pl.pallas_call(feed_kernel, name='feed', out_shape=(jax.ShapeDtypeStruct(...  59.8 us
    pallas_call x1, Pallas kernels, enter(): pl.pallas_call(enter_kernel, name='enter', out_shape=(jax.ShapeDtypeStruc...  44.3 us
    pallas_call x1, Pallas kernels, attend(): pl.pallas_call(attend_kernel, name='attend', out_shape=(jax.ShapeDtypeStr...  42.1 us
    unnamed x6, waiting for transfers between devices  40.3 us
  transfers between devices with their start and end apart: 5, of which 4 were waited for; matrix products, arithmetic and copies ran while one was open for 2% of the time, Pallas kernels for 0%

profile of v1, /device:TPU:0, one launch (start us, length us, event | category | flops | bytes accessed | tf_op | source)
XLA Modules:
  0.0 605.9 jit_solution(2467980851510555035)
XLA Ops:
  7.2 1.9 copy.39.tok
  9.1 1.9 copy.40.dout
  11.0 1.2 reshape.43.b_proj
  12.3 1.2 reshape.44.b_out
  13.5 2.2 copy.41.wo
  16.3 44.3 %enter.1 = (bf16[128,1280]{1,0:T(8,128)(2,1)}, bf16[128,1280]{1,0:T(8,128)(2,1)}, f32[8,1280]{1,0:T(8,128)}, bf16[512,1280]{1,0:T(8,128)(2,1)}, bf16[512,640]{1,...) custom-call(bf16[512,320]{1,0:T(8,128)(2,1)} %copy.39.tok, ...), custom_call_target="tpu_custom_call" | custom-call | tf_op jit(solution)/shard_map/enter/pallas_call | solution.py:186
  60.6 42.1 %attend.1 = (bf16[512,320]{1,0:T(8,128)(2,1)}, f32[32,128]{1,0:T(8,128)}, bf16[640,2048]{1,0:T(8,128)(2,1)}, f32[128,1280]{1,0:T(8,128)}, bf16[128,1280]{1,0:T(8...) custom-call(bf16[512,640]{1,0:T(8,128)(2,1)} %get-tuple-element.42.q, ...), custom_call_target="tpu_custom_call" | custom-call | tf_op jit(solution)/shard_map/attend/pallas_call | solution.py:316
  102.7 59.8 %feed.1 = (bf16[4,128,320]{2,1,0:T(8,128)(2,1)}, f32[128,1280]{1,0:T(8,128)}, bf16[128,1280]{1,0:T(8,128)(2,1)}, bf16[1280,1280]{1,0:T(8,128)(2,1)}, bf16[1280,1...) custom-call(bf16[128,1280]{1,0:T(8,128)(2,1)} %get-tuple-element.48.x2, ...), custom_call_target="tpu_custom_call" | custom-call | tf_op jit(solution)/shard_map/feed/pallas_call | solution.py:447
  162.5 60.5 %attend_back.1 = (bf16[512,960]{1,0:T(8,128)(2,1)}, bf16[4,320,320]{2,1,0:T(8,128)(2,1)}) custom-call(bf16[128,1280]{1,0:T(8,128)(2,1)} %get-tuple-element.54.gb, bf16[512,320]{1,0:T(8,128)(2,1)} %get-tuple-element.55.att, f32[32,128]{1,0:T(8,128)} %get-tuple-element.56.lse, bf16[512,640]{1,0:T(8,128)(2,1)} %get-tuple-element.42.q, ...), custom_call_target="tpu_custom_call" | custom-call | tf_op jit(solution)/shard_map/attend_back/pallas_call | solution.py:559
  223.0 34.0 %leave.1 = (bf16[4,128,320]{2,1,0:T(8,128)(2,1)}, bf16[1280,960]{1,0:T(8,128)(2,1)}, f32[2,320]{1,0:T(2,128)}, f32[8,1280]{1,0:T(8,128)}) custom-call(bf16[512,960]{1,0:T(8,128)(2,1)} %get-tuple-element.59.gmx, bf16[3,1280,320]{2,1,0:T(8,128)(2,1)} %get-tuple-element.60.wa, bf16[512,1280]{1,0:T(8,128)(2,1)} %get-tuple-element.61.x1, ...), custom_call_target="tpu_custom_call" | custom-call | tf_op jit(solution)/shard_map/leave/pallas_call | solution.py:636
  257.1 3.4 copy.47
  261.9 26.9 %reduce-scatter.7.cloned.1.call-done = bf16[320,960]{1,0:T(8,128)(2,1)} async-done(((bf16[1280,960]{1,0:T(8,128)(2,1)}), bf16[320,960]{1,0:T(8,128)(2,1)}) %reduce-scatter.7.cloned.1.call-update) | async-done | bytes 614416 | tf_op jit(solution)/shard_map/reduce_scatter | solution.py:668
  288.8 2.2 copy.42
  291.0 39.0 %reduce-scatter.13.cloned.1.call-done = bf16[320,1280]{1,0:T(8,128)(2,1)} async-done(((bf16[1280,1280]{1,0:T(8,128)(2,1)}), bf16[320,1280]{1,0:T(8,128)(2,1)}) %reduce-scatter.13.cloned.1.call-update) | async-done | bytes 819216
  330.0 2.3 copy.48
  332.3 21.1 %reduce-scatter.9.cloned.1.call-done = bf16[1,320,320]{2,1,0:T(8,128)(2,1)} async-done(((bf16[4,320,320]{2,1,0:T(8,128)(2,1)}), bf16[1,320,320]{2,1,0:T(8,128)(2,1)}) %reduce-scatter.9.cloned.1.call-update) | async-done | bytes 204816 | tf_op jit(solution)/shard_map/reduce_scatter | solution.py:668
  353.4 41.4 %reduce-scatter.11.cloned.1.call-done = bf16[320,1280]{1,0:T(8,128)(2,1)} async-done(((bf16[1280,1280]{1,0:T(8,128)(2,1)}), bf16[320,1280]{1,0:T(8,128)(2,1)}) %reduce-scatter.11.cloned.1.call-update) | async-done | bytes 819216 | tf_op jit(solution)/shard_map/reduce_scatter | solution.py:668
  395.7 0.9 copy.44
  396.6 0.9 copy.43
  397.5 131.2 %all-reduce = (f32[2,320]{1,0:T(2,128)}, f32[1280]{0:T(1024)}) all-reduce(f32[2,320]{1,0:T(2,128)S(1)} %copy-done.9, f32[1280]{0:T(1024)S(1)} %reduce.1), channel_id=1, replica_groups=mesh['dp'=8,'width'=4,'heads'=4] {'dp','width'}, use_global_device_ids=true, to_apply=%region_3.0 | all-reduce | flops 1920 | bytes 15360 | tf_op jit(solution)/shard_map/psum | solution.py:679
  528.7 63.0 %psum.49 = f32[6,1280]{1,0:T(8,128)S(1)} all-reduce(f32[6,1280]{1,0:T(8,128)S(1)} %pad_maximum_fusion), channel_id=1, replica_groups=mesh['dp'=8,'width'=4,'heads'=4] {'dp','heads','width'}, use_global_device_ids=true, to_apply=%region_0.0 | all-reduce | flops 7680 | bytes 61440 | tf_op jit(solution)/shard_map/psum | solution.py:674
  593.0 2.5 convert_element_type.8
  595.5 1.5 copy.46
  597.0 1.4 copy.45
  (39 shorter events, 5.0 us)
Async XLA Ops:
  7.2 8.5 %copy-start.7 = (f32[1280]{0:T(1024)S(1)}, f32[1280]{0:T(1024)}, u32[]{:S(2)}) copy-start(f32[1280]{0:T(1024)} %param.20) | copy-start | bytes 15364
  7.2 281.6 %reduce-scatter.7.cloned.1.call-start = ((), (), s32[]{:S(2)}) async-start(), calls=%async_computation.4 | async-start | bytes 3276800 | tf_op jit(solution)/shard_map/reduce_scatter | solution.py:668
  223.0 34.1 %copy-start = (bf16[1280,1280]{1,0:T(8,128)(2,1)S(1)}, bf16[1280,1280]{1,0:T(8,128)(2,1)}, u32[]{:S(2)}) copy-start(bf16[1280,1280]{1,0:T(8,128)(2,1)} %get-tuple-element.71) | copy-start | bytes 9830404
  257.0 73.0 %reduce-scatter.13.cloned.1.call-start = ((), (), s32[]{:S(2)}) async-start(), calls=%async_computation.7 | async-start | bytes 4096000
  260.5 92.9 %reduce-scatter.9.cloned.1.call-start = ((), (), s32[]{:S(2)}) async-start(), calls=%async_computation.5 | async-start | bytes 1228800 | tf_op jit(solution)/shard_map/reduce_scatter | solution.py:668
  261.3 133.6 %reduce-scatter.11.cloned.1.call-start = ((), (), s32[]{:S(2)}) async-start(), calls=%async_computation.6 | async-start | bytes 4096000 | tf_op jit(solution)/shard_map/reduce_scatter | solution.py:668
  261.8 331.1 %all-reduce.4.cloned.1.call-start = ((), (), s32[]{:S(2)}) async-start(), calls=%async_computation.8 | async-start | bytes 5570560 | tf_op jit(solution)/shard_map/psum | solution.py:673
  291.0 104.7 %copy-start.6 = (f32[8,1280]{1,0:T(8,128)S(1)}, f32[8,1280]{1,0:T(8,128)}, u32[]{:S(2)}) copy-start(f32[8,1280]{1,0:T(8,128)} %get-tuple-element.65) | copy-start | bytes 122884
  291.0 104.7 %copy-start.4 = (bf16[4,128,320]{2,1,0:T(8,128)(2,1)S(1)}, bf16[4,128,320]{2,1,0:T(8,128)(2,1)}, u32[]{:S(2)}) copy-start(bf16[4,128,320]{2,1,0:T(8,128)(2,1)} %get-tuple-element.63) | copy-start | bytes 983044
  330.0 66.6 %copy-start.3 = (bf16[4,128,320]{2,1,0:T(8,128)(2,1)S(1)}, bf16[4,128,320]{2,1,0:T(8,128)(2,1)}, u32[]{:S(2)}) copy-start(bf16[4,128,320]{2,1,0:T(8,128)(2,1)} %get-tuple-element.53) | copy-start | bytes 983044
  332.3 65.2 %copy-start.8 = (f32[1,1280]{1,0:T(1,128)S(1)}, f32[1,1280]{1,0:T(1,128)}, u32[]{:S(2)}) copy-start(f32[1,1280]{1,0:T(1,128)} %get-tuple-element.70) | copy-start | bytes 15364
  332.3 65.2 %copy-start.9 = (f32[2,320]{1,0:T(2,128)S(1)}, f32[2,320]{1,0:T(2,128)}, u32[]{:S(2)}) copy-start(f32[2,320]{1,0:T(2,128)} %get-tuple-element.67) | copy-start | bytes 7684
  593.0 2.6 copy-start.1
  593.0 4.0 copy-start.2
  595.5 2.9 copy-start.5
Sparse Core Ops, SparseCore 0:
  257.2 31.5 reduce-scatter.6
  291.2 38.7 reduce-scatter.12
  332.5 20.9 reduce-scatter.8
  355.9 38.9 reduce-scatter.10
  398.9 99.0 all-reduce.3

commit v2 on v0

v2 whole, which is shorter than its diff:
```python
import functools

import jax
import jax.numpy as jnp
from jax import lax
from jax.experimental import pallas as pl
from jax.experimental.pallas import tpu as pltpu
from jax.sharding import PartitionSpec as P

F32, BF16 = jnp.float32, jnp.bfloat16
D, HS, ROWS, PART, QUARTER, HEADS = 1280, 64, 128, 320, 512, 5
PAIR = 2 * PART
STRIP = PART // 4
HALF = ROWS // 2
EPSILON = 1e-05
GELU_COEF = 0.7978845608028654
MASKED = -1e30
VMEM = pl.BlockSpec(memory_space=pltpu.VMEM)
ANY = pl.BlockSpec(memory_space=pl.ANY)
TILES = D // 256


def nn(a, b):
    return jnp.dot(a, b, preferred_element_type=F32)


def nt(a, b):
    return lax.dot_general(a, b, (((1,), (1,)), ((), ())), preferred_element_type=F32)


def tn(a, b):
    return lax.dot_general(a, b, (((0,), (0,)), ((), ())), preferred_element_type=F32)


def rows_of(start, size=ROWS):
    return pl.ds(pl.multiple_of(start, size), size)


def block_of(who):
    return pl.ds(pl.multiple_of(who * PART, 64), PART)


def tile_of(i, size):
    return pl.ds(pl.multiple_of(i * size, size), size)


def sub_block(quarter, w):
    return w + lax.rem(quarter, 2) * (3 - 2 * w)


class Place:
    def __init__(self):
        self.dp, self.w, self.h = (lax.axis_index(n) for n in ("dp", "width", "heads"))
        self.x = lax.rem(self.dp, 4)
        self.wc = self.w + 1 - 2 * lax.rem(self.w, 2)
        self.wy = lax.rem(self.w + 2, 4)
        self.wyc = lax.rem(self.wc + 2, 4)
        across = lax.rem(self.dp + 4, 8)
        self.core = (self.dp, self.wc, self.h)
        self.near = (self.dp, self.wy, self.h)
        self.near_core = (self.dp, self.wyc, self.h)
        self.far = (across, self.wy, self.h)
        self.opposite = (across, self.w, self.h)
        self.width_peers = ((self.near, self.wy), (self.near_core, self.wyc), (self.core, self.wc))

    def along_z(self, k):
        return (self.dp, self.w, lax.rem(self.h + k, 4))

    def along_x(self, k):
        return (self.dp - self.x + lax.rem(self.x + k, 4), self.w, self.h)

    def chunk(self, k):
        return lax.rem(self.h + k, 4)


def greet(devices):
    barrier = pltpu.get_barrier_semaphore()
    for device in devices:
        pl.semaphore_signal(barrier, inc=1, device_id=device, device_id_type=pl.DeviceIdType.MESH)
    pl.semaphore_wait(barrier, len(devices))


class Move:
    def __init__(self, copy):
        self.copy, self.left = copy, False
        self.start, self.wait_recv = copy.start, copy.wait_recv

    def wait_send(self):
        if not self.left:
            self.copy.wait_send()
        self.left = True

    def wait(self):
        self.wait_recv()
        self.wait_send()


class Links:
    def __init__(self, sent, landed):
        self.sent, self.landed, self.copies = sent, landed, []

    def plan(self, source, target, device):
        i = len(self.copies)
        copy = pltpu.make_async_remote_copy(
            src_ref=source,
            dst_ref=target,
            send_sem=self.sent.at[i],
            recv_sem=self.landed.at[i],
            device_id=device,
            device_id_type=pl.DeviceIdType.MESH,
        )
        self.copies.append(Move(copy))
        return self.copies[-1]

    def send(self, source, target, device):
        copy = self.plan(source, target, device)
        copy.start()
        return copy


class GatherZ:
    def __init__(self, links, at, source, rows):
        self.links, self.at, self.rows = links, at, rows
        own = rows.at[rows_of(at.h * ROWS)]
        self.right = links.send(source, own, at.along_z(1))
        self.left = links.send(source, own, at.along_z(3))
        low = rows.at[rows_of(at.chunk(3) * ROWS, HALF)]
        high = rows.at[rows_of(at.chunk(1) * ROWS + HALF, HALF)]
        self.low = links.plan(low, low, at.along_z(1))
        self.high = links.plan(high, high, at.along_z(3))

    def neighbours(self):
        self.left.wait_recv()
        self.high.start()
        self.right.wait_recv()
        self.low.start()

    def rest(self):
        self.low.wait_recv()
        self.high.wait_recv()


class SumZ:
    def __init__(self, links, at, stage, parts, over):
        self.stage, self.parts, self.over, self.at = stage, parts, over, at
        ahead, behind, across = at.chunk(1), at.chunk(3), at.chunk(2)
        right, left = at.along_z(1), at.along_z(3)
        top, bottom = pl.ds(0, HALF), pl.ds(HALF, HALF)
        self.ahead, self.behind = ahead, behind
        self.far_right = links.plan(stage.at[across, top], over.at[0], right)
        self.far_left = links.plan(stage.at[across, bottom], over.at[1], left)
        self.right_bottom = links.plan(stage.at[ahead, bottom], parts.at[0, bottom], right)
        self.right_top = links.plan(stage.at[ahead, top], parts.at[0, top], right)
        self.left_top = links.plan(stage.at[behind, top], parts.at[1, top], left)
        self.left_bottom = links.plan(stage.at[behind, bottom], parts.at[1, bottom], left)

    def sent(self):
        for copy in (self.far_right, self.far_left, self.right_bottom, self.right_top, self.left_top, self.left_bottom):
            copy.wait_send()

    def send_across(self):
        self.far_right.start()
        self.far_left.start()

    def send_ahead(self):
        self.right_bottom.start()
        self.far_right.wait_recv()
        joined = self.stage[self.ahead, 0:HALF, :].astype(F32) + self.over[0].astype(F32)
        self.stage[self.ahead, 0:HALF, :] = joined.astype(BF16)
        self.right_top.start()

    def send_behind(self):
        self.left_top.start()
        self.far_left.wait_recv()
        joined = self.stage[self.behind, HALF:, :].astype(F32) + self.over[1].astype(F32)
        self.stage[self.behind, HALF:, :] = joined.astype(BF16)
        self.left_bottom.start()

    def result(self):
        for copy in (self.right_bottom, self.right_top, self.left_top, self.left_bottom):
            copy.wait_recv()
        return self.stage[self.at.h].astype(F32) + self.parts[0].astype(F32) + self.parts[1].astype(F32)


class GradientSum:
    def __init__(self, links, at, grad, columns, pair, strips, cross, final):
        self.links, self.at, self.grad, self.columns = links, at, grad, columns
        self.pair, self.strips, self.cross, self.final = pair, strips, cross, final
        self.strip = rows_of(at.x * STRIP, STRIP)
        self.total = [pair.at[0, self.strip], pair.at[1, self.strip]]

    def mine(self, who):
        return self.grad.at[block_of(who), self.columns]

    def send_core(self):
        at, links = self.at, self.links
        self.core = [
            links.send(self.mine(at.wc), self.pair.at[0], at.core),
            links.send(self.mine(at.wyc), self.pair.at[1], at.core),
        ]

    def send_x(self):
        at, links = self.at, self.links
        for i, who in ((0, at.w), (1, at.wy)):
            self.core[i].wait()
            self.pair[i] = (self.pair[i].astype(F32) + self.mine(who)[...].astype(F32)).astype(BF16)
        self.along = [
            links.send(
                self.pair.at[:, rows_of(lax.rem(at.x + k, 4) * STRIP, STRIP)], self.strips.at[k - 1], at.along_x(k)
            )
            for k in (2, 1, 3)
        ]

    def send_y(self):
        at, links = self.at, self.links
        for copy in self.along:
            copy.wait()
        for i in range(2):
            joined = self.total[i][...].astype(F32)
            for k in range(3):
                joined = joined + self.strips[k, i].astype(F32)
            self.total[i][...] = joined.astype(BF16)
        self.over = [
            links.send(self.total[1], self.cross.at[0], at.near),
            links.send(self.total[1], self.cross.at[1], at.far),
            links.send(self.total[0], self.cross.at[2], at.opposite),
        ]

    def send_back(self):
        at, links = self.at, self.links
        for copy in self.over:
            copy.wait()
        joined = self.total[0][...].astype(F32)
        for k in range(3):
            joined = joined + self.cross[k].astype(F32)
        self.total[0][...] = joined.astype(BF16)
        strip = self.final.at[self.strip]
        self.back = [links.send(self.total[0], strip, at.along_x(k)) for k in (2, 1, 3)]
        return strip

    def finish(self):
        for copy in self.back:
            copy.wait()


def norm_stats(values):
    mean = jnp.mean(values, axis=1, keepdims=True)
    centred = values - mean
    scale = lax.rsqrt(jnp.mean(centred * centred, axis=1, keepdims=True) + EPSILON)
    return centred * scale, scale


def norm_gradient(grad, unit, scale, gain):
    scaled = grad * gain
    mean = jnp.mean(scaled, axis=1, keepdims=True)
    along = jnp.mean(scaled * unit, axis=1, keepdims=True)
    return scale * (scaled - mean - unit * along)


def interleave(first, second):
    pieces = []
    for head in range(HEADS):
        part = slice(head * HS, (head + 1) * HS)
        pieces += [first[:, part], second[:, part]]
    return jnp.concatenate(pieces, axis=1)


def visible_scores(scores, quarter, shift):
    last = scores[quarter * QUARTER :]
    key = lax.broadcasted_iota(jnp.int32, last.shape, 0)
    query = lax.broadcasted_iota(jnp.int32, last.shape, 1) + shift
    last = jnp.where(key <= query, last, MASKED)
    return last if quarter == 0 else jnp.concatenate([scores[: quarter * QUARTER], last], axis=0)


def column_sum(values):
    return jnp.sum(values, axis=0, keepdims=True)


SCRATCH = dict(
    wkv=((D, PAIR), BF16),
    wq=((D, PART), BF16),
    wpt=((D, PART), BF16),
    wf=((D, D), BF16),
    wt=((D, D), BF16),
    wa_raw=((3, PART, PART), BF16),
    wp_raw=((PART, PART), BF16),
    wo_raw=((D, PART), BF16),
    xa=((4, ROWS, PART), BF16),
    da=((4, ROWS, PART), BF16),
    vl=((8, PART), F32),
    vg=((4, 8, PART), F32),
    vec=((8, D), F32),
    bf=((8, D), F32),
    x=((ROWS, D), BF16),
    x1=((QUARTER, D), BF16),
    q=((QUARTER, PAIR), BF16),
    kv=((2048, PAIR), BF16),
    kvt=((PAIR, 2048), BF16),
    att=((QUARTER, PART), BF16),
    att_t=((PART, ROWS), F32),
    lse=((32, 128), F32),
    middle=((ROWS, D), F32),
    stage=((4, ROWS, D), BF16),
    parts=((2, ROWS, D), BF16),
    over=((2, HALF, D), BF16),
    d_all=((QUARTER, D), BF16),
    x2=((QUARTER, D), BF16),
    hid=((QUARTER, D), BF16),
    gp=((QUARTER, D), BF16),
    stage_g=((4, ROWS, D), BF16),
    parts_g=((3, ROWS, D), BF16),
    parts_b=((2, ROWS, D), BF16),
    over_b=((2, HALF, D), BF16),
    back=((4, ROWS, PART), BF16),
    gm=((ROWS, D), F32),
    grad_f=((D, D), BF16),
    grad_t=((D, D), BF16),
    pair_f=((2, PART, D), BF16),
    pair_t=((2, PART, D), BF16),
    pair_q=((2, PART, PAIR), BF16),
    pair_k=((2, PART, PAIR), BF16),
    strips_f=((3, 2, STRIP, D), BF16),
    strips_t=((3, 2, STRIP, D), BF16),
    strips_q=((3, 2, STRIP, PAIR), BF16),
    strips_k=((3, 2, STRIP, PAIR), BF16),
    cross_f=((3, STRIP, D), BF16),
    cross_t=((3, STRIP, D), BF16),
    cross_q=((3, STRIP, PAIR), BF16),
    cross_k=((3, STRIP, PAIR), BF16),
    g_all=((QUARTER, D), BF16),
    go=((ROWS, PAIR), BF16),
    dkv=((2048, PAIR), F32),
    take=((2, 4, ROWS, PAIR), BF16),
    take_y=((QUARTER, PAIR), BF16),
    dq=((QUARTER, PART), BF16),
    gkv=((QUARTER, PAIR), BF16),
    sums=((16, D), F32),
    sums_z=((3, 8, D), F32),
    sums_w=((4, 8, PART), F32),
    take_w=((3, 8, PART), F32),
    take_v=((3, 8, D), F32),
    sums_d=((8, D), F32),
    sums_x=((3, 8, D), F32),
    sums_o=((8, D), F32),
)
COPIES = 160


def block_kernel(*refs):
    names = ("tok", "dout", "gain", "shift", "b_proj", "b_out", "wa_in", "bqv", "wp_in", "wf_in", "b_fc", "wo_in")
    names += ("bo", "dt", "fin_f", "fin_t", "fin_q", "fin_k", "fin_v")
    names += tuple(SCRATCH) + ("sent", "landed", "local")
    r = dict(zip(names, refs))
    (tok, dout, gain, shift, b_proj, b_out, wa_in, bqv, wp_in, wf_in, b_fc, wo_in) = refs[:12]
    (bo, dt, fin_f, fin_t, fin_q, fin_k, fin_v) = refs[12:19]
    at = Place()
    w, h = at.w, at.h
    links = Links(r["sent"], r["landed"])
    local = r["local"]
    own = rows_of(h * ROWS)
    mine = sub_block(h, w)
    vec = r["vec"]

    loads = [
        pltpu.make_async_copy(wa_in, r["wa_raw"], local.at[0]),
        pltpu.make_async_copy(wp_in, r["wp_raw"], local.at[1]),
        pltpu.make_async_copy(wo_in, r["wo_raw"], local.at[2]),
        pltpu.make_async_copy(wf_in, r["wf"].at[block_of(w)], local.at[3]),
        pltpu.make_async_copy(tok.at[rows_of(mine * ROWS)], r["xa"].at[w], local.at[4]),
        pltpu.make_async_copy(dout.at[rows_of(mine * ROWS)], r["da"].at[w], local.at[5]),
    ]
    for copy in loads:
        copy.start()
    vl = r["vl"]
    vl[0:2, :] = gain[...]
    vl[2:4, :] = shift[...]
    vl[4:5, :] = b_proj[...].reshape(1, PART)
    vl[5:6, :] = b_out[...].reshape(1, PART)
    r["bf"][0:1, :] = b_fc[...].reshape(1, D)
    vl[6:8, :] = jnp.zeros((2, PART), F32)
    greet(
        [at.core, at.near, at.near_core, at.far, at.opposite]
        + [at.along_z(k) for k in (1, 2, 3)]
        + [at.along_x(k) for k in (1, 2, 3)]
    )

    def spread(source, slots):
        return [
            links.send(source.at[rows_of(sub_block(h, peer) * ROWS)], slots.at[w], device)
            for device, peer in at.width_peers
        ]

    arrive = spread(tok, r["xa"])
    arrive += [links.send(vl, r["vg"].at[w], device) for device, _ in at.width_peers]
    r["vg"][w] = vl[...]

    class Weight:
        def __init__(self, full, start=True):
            own_block, next_block = full.at[block_of(w)], full.at[block_of(at.wy)]
            self.far = links.plan(own_block, own_block, at.far)
            self.core = links.plan(own_block, own_block, at.core)
            self.other = links.plan(next_block, next_block, at.core)
            if start:
                self.start()

        def start(self):
            self.far.start()
            self.core.start()

        def forward(self):
            self.far.wait_recv()
            self.other.start()

        def ready(self):
            self.core.wait_recv()
            self.other.wait_recv()

    loads[0].wait()
    r["wkv"][block_of(w), :] = interleave(r["wa_raw"][1], r["wa_raw"][2])
    weight_kv = Weight(r["wkv"])
    r["wq"][block_of(w), :] = r["wa_raw"][0]
    weight_q = Weight(r["wq"])
    loads[1].wait()
    r["wpt"][block_of(w), :] = r["wp_raw"][...].T
    weight_p = Weight(r["wpt"])

    loads[4].wait()
    for copy in arrive:
        copy.wait_recv()
    vec[...] = jnp.concatenate([r["vg"][i] for i in range(4)], axis=1)
    r["x"][...] = jnp.concatenate([r["xa"][i] for i in range(4)], axis=1)
    unit, _ = norm_stats(r["x"][...].astype(F32))
    x1, kv, q = r["x1"], r["kv"], r["q"]
    x1[own, :] = (unit * vec[0:1, :] + vec[2:3, :]).astype(BF16)
    gather = GatherZ(links, at, x1.at[own], x1)
    loads[2].wait()
    r["wt"][block_of(w), :] = r["wo_raw"][...].T
    loads[3].wait()
    weight_kv.forward()
    weight_kv.ready()
    value_bias = interleave(jnp.zeros((1, PART), F32), bqv[1:2, :])

    def key_block(c, who):
        return kv.at[rows_of((c * 4 + sub_block(c, who)) * ROWS)]

    shares, passed = [], []
    order = [at.chunk(k) for k in (0, 1, 3, 2)]
    for i, c in enumerate(order):
        if i == 1:
            gather.neighbours()
        if i == 3:
            gather.rest()
        key_block(c, w)[...] = (nn(x1[rows_of(c * ROWS), :], r["wkv"][...]) + value_bias).astype(BF16)
        shares.append(links.send(key_block(c, w), key_block(c, w), at.near))
        shares.append(links.send(key_block(c, w), key_block(c, w), at.core))
    weight_t = Weight(r["wt"])
    weight_f = Weight(r["wf"])
    weight_q.forward()
    weight_p.forward()
    weight_q.ready()
    queries = (nn(x1[...], r["wq"][...]) + bqv[0:1, :]).astype(BF16).astype(F32) * HS**-0.5
    q[...] = interleave(queries.astype(BF16), jnp.zeros((QUARTER, PART), BF16))
    for i, c in enumerate(order):
        shares[2 * i].wait_recv()
        passed.append(links.send(key_block(c, at.wy), key_block(c, at.wy), at.core))
    arrive_d = spread(dout, r["da"])
    for i in range(4):
        shares[2 * i + 1].wait_recv()
        passed[i].wait_recv()

    kvt, att, lse, d_all = r["kvt"], r["att"], r["lse"], r["d_all"]

    @pl.loop(0, HEADS)
    def _(head):
        kvt[tile_of(head, 128), :] = kv[:, tile_of(head, 128)].T

    weight_p.ready()
    loads[5].wait()
    for copy in arrive_d:
        copy.wait_recv()
    d_all[own, :] = jnp.concatenate([r["da"][i] for i in range(4)], axis=1)
    gather_d = GatherZ(links, at, d_all.at[own], d_all)
    stage = r["stage"]
    sum_p = SumZ(links, at, stage, r["parts"], r["over"])

    def attend_chunk(j):
        keys = (j + 1) * QUARTER
        shift = sub_block(j, w) * ROWS

        @pl.loop(0, HEADS)
        def _(head):
            tile = tile_of(head, 128)
            scores = visible_scores(nt(kv[0:keys, tile], q[j * ROWS : (j + 1) * ROWS, tile]), j, shift)
            peak = jnp.max(scores, axis=0, keepdims=True)
            weights = jnp.exp(scores - peak)
            total = column_sum(weights)
            probs = (weights * (1.0 / total)).astype(BF16)
            r["att_t"][tile_of(head, HS), :] = nn(kvt[tile, 0:keys], probs)[HS:, :]
            lse[pl.ds(j * 8 + head, 1), :] = peak + jnp.log(total)

    @pl.loop(0, 4)
    def _(i):
        j = at.chunk(jnp.where(i == 0, 2, jnp.where(i == 3, 0, 2 * i - 1)))
        for case in range(4):
            pl.when(j == case)(functools.partial(attend_chunk, case))
        attended = r["att_t"][...].T.astype(BF16)
        att[rows_of(j * ROWS), :] = attended
        stage[j] = nt(attended, r["wpt"][...]).astype(BF16)
        pl.when(i == 0)(sum_p.send_across)
        pl.when(i == 0)(gather_d.neighbours)
        pl.when(i == 1)(sum_p.send_ahead)
        pl.when(i == 2)(sum_p.send_behind)

    gather_d.rest()
    weight_t.forward()
    weight_f.forward()
    middle = r["x"][...].astype(F32) + vec[4:5, :] + sum_p.result()
    r["middle"][...] = middle
    unit, _ = norm_stats(middle)
    x2, hid, gp = r["x2"], r["hid"], r["gp"]
    x2[own, :] = (unit * vec[1:2, :] + vec[3:4, :]).astype(BF16)

    gather = GatherZ(links, at, x2.at[own], x2)
    weight_t.ready()
    weight_f.ready()
    wf, wt = r["wf"], r["wt"]
    hidden_grad = r["dkv"]
    stage_g, parts_g = r["stage_g"], r["parts_g"]

    @pl.loop(0, TILES)
    def _(t):
        grad = nn(d_all[...], wt[:, tile_of(t, 256)])
        hidden_grad[rows_of(t // 2 * QUARTER, QUARTER), tile_of(t - t // 2 * 2, 256)] = grad

    moves = []
    for i, c in enumerate(order):
        if i == 1:
            gather.neighbours()
        if i == 3:
            gather.rest()
        rows = rows_of(c * ROWS)

        @pl.loop(0, TILES)
        def _(t):
            tile = tile_of(t, 256)
            u = nn(x2[rows, :], wf[:, tile]) + r["bf"][0:1, tile]
            square = u * u
            th = jnp.tanh(GELU_COEF * (u + 0.044715 * square * u))
            hid[rows, tile] = (0.5 * u * (1.0 + th)).astype(BF16)
            slope = 0.5 * (1.0 + th) + 0.5 * u * (1.0 - th * th) * (GELU_COEF * (1.0 + 0.134145 * square))
            grad = hidden_grad[rows_of(t // 2 * QUARTER + c * ROWS), tile_of(t - t // 2 * 2, 256)]
            gp[rows, tile] = (grad * slope).astype(BF16)

        @pl.loop(0, TILES)
        def _(t):
            stage_g[c, :, tile_of(t, 256)] = nt(gp[rows, :], wf[tile_of(t, 256), :]).astype(BF16)

        if i:
            moves.append(links.send(stage_g.at[c], parts_g.at[i - 1], at.along_z((0, 1, 3, 2)[i])))

    sum_p.sent()
    sum_b = SumZ(links, at, stage, r["parts_b"], r["over_b"])

    @pl.loop(0, TILES)
    def _(t):
        product = nt(hid[...], wt[tile_of(t, 256), :]).astype(BF16)
        for c in range(4):
            stage[c, :, tile_of(t, 256)] = product[c * ROWS : (c + 1) * ROWS]

    sum_b.send_across()
    grad_f, grad_t = r["grad_f"], r["grad_t"]

    @pl.loop(0, TILES)
    def _(t):
        grad_t[tile_of(t, 256), :] = tn(d_all[:, tile_of(t, 256)], hid[...]).astype(BF16)

    def gradient_sum(tag, grad, columns, final):
        return GradientSum(
            links, at, grad, columns, r["pair_" + tag], r["strips_" + tag], r["cross_" + tag], final
        )

    whole = slice(0, D)
    sum_t = gradient_sum("t", grad_t, whole, fin_t)
    sum_t.send_core()

    @pl.loop(0, TILES)
    def _(t):
        grad_f[tile_of(t, 256), :] = tn(x2[:, tile_of(t, 256)], gp[...]).astype(BF16)

    sum_f = gradient_sum("f", grad_f, whole, fin_f)
    sum_f.send_core()
    sums = r["sums"]
    sums[8:9, :] = column_sum(gp[...].astype(F32))
    unit, scale = norm_stats(r["middle"][...])
    grad = d_all[own, :].astype(F32)
    grad_normed = stage_g[h].astype(F32)
    for i in range(3):
        moves[i].wait_recv()
        grad_normed = grad_normed + parts_g[i].astype(F32)
    grad_middle = grad + norm_gradient(grad_normed, unit, scale, vec[1:2, :])
    r["gm"][...] = grad_middle
    branch = grad_middle.astype(BF16)
    g_all = r["g_all"]
    g_all[own, :] = branch
    gather = GatherZ(links, at, g_all.at[own], g_all)
    sums[1:2, :] = column_sum(grad_normed * unit)
    sums[3:4, :] = column_sum(grad_normed)
    sums[4:5, :] = column_sum(grad)
    sums[5:6, :] = column_sum(branch.astype(F32))
    sum_b.send_ahead()
    sum_b.send_behind()
    sum_t.send_x()
    sum_f.send_x()

    def send_rows(result, target):
        result = result.astype(BF16)
        back = r["back"]
        for part in range(4):
            back[part] = result[:, part * PART : (part + 1) * PART]
        keep = pltpu.make_async_copy(back.at[w], target.at[mine], local.at[6])
        keep.start()
        copies = [links.send(back.at[peer], target.at[mine], device) for device, peer in at.width_peers]
        keep.wait()
        return copies

    dkv, go, dq = r["dkv"], r["go"], r["dq"]
    dkv[...] = jnp.zeros(dkv.shape, F32)
    zeros = jnp.zeros((ROWS, PART), BF16)

    def back_chunk(j):
        keys = (j + 1) * QUARTER
        shift = sub_block(j, w) * ROWS
        rows = slice(j * ROWS, (j + 1) * ROWS)

        @pl.loop(0, HEADS)
        def _(head):
            tile = tile_of(head, 128)
            query, grad = q[rows, tile], go[:, tile]
            scores = visible_scores(nt(kv[0:keys, tile], query), j, shift)
            probs = jnp.exp(scores - lse[pl.ds(j * 8 + head, 1), :])
            grad_probs = nt(kv[0:keys, tile], grad)
            inner = column_sum(grad_probs * probs)
            grad_scores = (probs * (grad_probs - inner)).astype(BF16)
            both = jnp.concatenate([grad_scores, probs.astype(BF16)], axis=1)
            dkv[0:keys, tile] += nn(both, jnp.concatenate([query, grad], axis=0))
            r["att_t"][tile_of(head, HS), :] = nn(kvt[tile, 0:keys], grad_scores)[:HS, :] * HS**-0.5

    @pl.loop(0, 4)
    def _(i):
        pl.when(i == 1)(gather.neighbours)
        pl.when(i == 3)(gather.rest)
        c = at.chunk(jnp.where(i == 2, 3, jnp.where(i == 3, 2, i)))
        rows = rows_of(c * ROWS)
        go[...] = interleave(zeros, nn(g_all[rows, :], r["wpt"][...]).astype(BF16))
        for case in range(4):
            pl.when(c == case)(functools.partial(back_chunk, case))
        dq[rows, :] = r["att_t"][...].T.astype(BF16)

    def piece(who, j):
        return dkv[rows_of((j * 4 + sub_block(j, who)) * ROWS), :]

    take, take_y, gkv = r["take"], r["take_y"], r["gkv"]
    halves = (slice(0, PAIR), slice(PAIR, D))
    for copy in moves:
        copy.wait_send()
    quarters = [slice(j * ROWS, (j + 1) * ROWS) for j in range(4)]
    for j in range(4):
        stage_g[j, :, halves[1]] = piece(at.wyc, j).astype(BF16)
    first = links.send(stage_g.at[:, :, halves[1]], take.at[1], at.core)
    for j in range(4):
        stage_g[j, :, halves[0]] = piece(at.wc, j).astype(BF16)
    second = links.send(stage_g.at[:, :, halves[0]], take.at[0], at.core)
    first.wait_recv()
    for j in range(4):
        gkv[quarters[j], :] = (piece(at.wy, j) + take[1, j].astype(F32)).astype(BF16)
    third = links.send(gkv, take_y, at.near)

    @pl.loop(0, TILES)
    def _(t):
        tile = tile_of(t, 256)
        pieces = [tn(x1[:, tile], dq[...]).astype(BF16), tn(g_all[:, tile], att[...]).astype(BF16)]
        grad_t[tile, PAIR:] = jnp.concatenate(pieces, axis=1)

    sum_q = gradient_sum("q", grad_t, slice(PAIR, D), fin_q)
    sum_q.send_core()
    result = r["middle"][...] + vec[5:6, :] + sum_b.result()
    returns = send_rows(result, bo)
    sums[9:10, 0:PART] = column_sum(dq[...].astype(F32))
    second.wait_recv()
    third.wait()
    for j in range(4):
        total = piece(w, j) + take[0, j].astype(F32) + take_y[quarters[j], :].astype(F32)
        gkv[quarters[j], :] = total.astype(BF16)

    sum_b.sent()
    sum_l = SumZ(links, at, stage, r["parts"], r["over"])

    def first_partial(k):
        c = at.chunk(k)
        rows = rows_of(c * ROWS)
        stage[c] = (nt(dq[rows, :], r["wq"][...]) + nt(gkv[rows, :], r["wkv"][...])).astype(BF16)

    first_partial(2)
    sum_l.send_across()
    first_partial(1)
    first_partial(3)
    sum_l.send_ahead()
    sum_l.send_behind()

    @pl.loop(0, TILES)
    def _(t):
        tile = tile_of(t, 256)
        grad_t[tile, 0:PAIR] = tn(x1[:, tile], gkv[...]).astype(BF16)

    sum_k = gradient_sum("k", grad_t, slice(0, PAIR), fin_k)
    sum_k.send_core()
    first_partial(0)
    sum_q.send_x()
    sum_t.send_y()
    sum_f.send_y()
    sum_k.send_x()
    grad_values = column_sum(gkv[...].astype(F32))
    for head in range(HEADS):
        sums[9:10, PART + head * HS : PART + (head + 1) * HS] = grad_values[:, head * 128 + HS : (head + 1) * 128]
    sums[9:10, PAIR:] = jnp.zeros((1, PAIR), F32)
    sums[10:16, :] = jnp.zeros((6, D), F32)
    sums[6:8, :] = jnp.zeros((2, D), F32)
    grad_normed = sum_l.result()
    unit, scale = norm_stats(r["x"][...].astype(F32))
    sums[0:1, :] = column_sum(grad_normed * unit)
    sums[2:3, :] = column_sum(grad_normed)
    over_z = [links.send(sums.at[0:8], r["sums_z"].at[k - 1], at.along_z(k)) for k in (1, 2, 3)]
    over_w = [links.send(sums.at[8:16], r["take_v"].at[i], at.width_peers[i][0]) for i in range(3)]
    result = r["gm"][...] + norm_gradient(grad_normed, unit, scale, vec[0:1, :])
    for copy in returns:
        copy.wait()
    returns = send_rows(result, dt)

    keep = []

    def send_back(total):
        strip = total.send_back()
        copy = pltpu.make_async_copy(total.total[0], strip, local.at[7 + len(keep)])
        copy.start()
        keep.append(copy)

    send_back(sum_t)
    send_back(sum_f)
    for copy in over_z + over_w:
        copy.wait()
    normed = sums[0:8, :] + r["sums_z"][0] + r["sums_z"][1] + r["sums_z"][2]
    for part in range(4):
        r["sums_w"][part] = normed[:, part * PART : (part + 1) * PART]
    over_w = [links.send(r["sums_w"].at[peer], r["take_w"].at[i], at.width_peers[i][0]) for i, (_, peer) in enumerate(at.width_peers)]
    biases = sums[8:10, :] + r["take_v"][0, 0:2] + r["take_v"][1, 0:2] + r["take_v"][2, 0:2]
    sum_q.send_y()
    for copy in over_w:
        copy.wait()
    sums_d = r["sums_d"]
    normed = r["sums_w"][w] + r["take_w"][0] + r["take_w"][1] + r["take_w"][2]
    sums_d[...] = jnp.zeros((8, D), F32)
    for i in range(6):
        sums_d[i // 3 : i // 3 + 1, (i % 3) * 384 : (i % 3) * 384 + PART] = normed[i : i + 1, :]
    sums_d[2:4, :] = biases
    over_x = [links.send(sums_d, r["sums_x"].at[k - 1], at.along_x(k)) for k in (1, 2, 3)]
    sum_k.send_y()
    for copy in over_x:
        copy.wait()
    sums_d[...] = sums_d[...] + r["sums_x"][0] + r["sums_x"][1] + r["sums_x"][2]
    over_o = links.send(sums_d, r["sums_o"], at.opposite)
    send_back(sum_q)
    send_back(sum_k)
    over_o.wait()
    fin_v[...] = sums_d[...] + r["sums_o"][...]
    for copy in keep:
        copy.wait()
    for total in (sum_t, sum_f, sum_q, sum_k):
        total.finish()
    for copy in returns:
        copy.wait()
    for copy in links.copies:
        copy.wait_send()


def block(*inputs):
    return pl.pallas_call(
        block_kernel,
        name="block",
        out_shape=(
            jax.ShapeDtypeStruct((4, ROWS, PART), BF16),
            jax.ShapeDtypeStruct((4, ROWS, PART), BF16),
            jax.ShapeDtypeStruct((PART, D), BF16),
            jax.ShapeDtypeStruct((PART, D), BF16),
            jax.ShapeDtypeStruct((PART, PAIR), BF16),
            jax.ShapeDtypeStruct((PART, PAIR), BF16),
            jax.ShapeDtypeStruct((8, D), F32),
        ),
        in_specs=[ANY, ANY, VMEM, VMEM, VMEM, VMEM, ANY, VMEM, ANY, ANY, VMEM, ANY],
        out_specs=(ANY, ANY, ANY, ANY, ANY, ANY, VMEM),
        scratch_shapes=[pltpu.VMEM(shape, kind) for shape, kind in SCRATCH.values()]
        + [pltpu.SemaphoreType.DMA((COPIES,)), pltpu.SemaphoreType.DMA((COPIES,)), pltpu.SemaphoreType.DMA((12,))],
        compiler_params=pltpu.CompilerParams(collective_id=1, has_side_effects=True, vmem_limit_bytes=64 * 2**20),
    )(*inputs)


def finish_kernel(bo, dt, f, t, qp, kv, v, out, d_tok, gain, shift, d_wa, d_bqv, d_wp, d_bp, d_wf, d_bf, d_wo, d_bo):
    for part in range(4):
        out[part * ROWS : (part + 1) * ROWS, :] = bo[part]
        d_tok[part * ROWS : (part + 1) * ROWS, :] = dt[part]
    d_wf[...] = f[...].astype(F32)
    d_wo[...] = t[...].astype(F32).T
    d_wa[0] = qp[:, :PART].astype(F32)
    d_wp[...] = qp[:, PART:].astype(F32).T
    both = kv[...].astype(F32)
    d_wa[1] = jnp.concatenate([both[:, head * 128 : head * 128 + HS] for head in range(HEADS)], axis=1)
    d_wa[2] = jnp.concatenate([both[:, head * 128 + HS : (head + 1) * 128] for head in range(HEADS)], axis=1)
    rows = [v[i // 3 : i // 3 + 1, (i % 3) * 384 : (i % 3) * 384 + PART] for i in range(6)]
    gain[0:1, :] = rows[0]
    gain[1:2, :] = rows[1]
    shift[0:1, :] = rows[2]
    shift[1:2, :] = rows[3]
    d_bo[...] = rows[4].reshape(PART)
    d_bp[...] = rows[5].reshape(PART)
    d_bf[...] = v[2:3, :].reshape(D)
    d_bqv[0:1, :] = v[3:4, 0:PART]
    d_bqv[1:2, :] = v[3:4, PART:PAIR]


def finish(*inputs):
    shapes = [
        ((QUARTER, PART), BF16),
        ((QUARTER, PART), BF16),
        ((2, PART), F32),
        ((2, PART), F32),
        ((3, PART, PART), F32),
        ((2, PART), F32),
        ((PART, PART), F32),
        ((PART,), F32),
        ((PART, D), F32),
        ((D,), F32),
        ((D, PART), F32),
        ((PART,), F32),
    ]
    return pl.pallas_call(
        finish_kernel,
        name="finish",
        out_shape=[jax.ShapeDtypeStruct(shape, kind) for shape, kind in shapes],
        in_specs=[VMEM] * 7,
        out_specs=[VMEM] * 12,
        compiler_params=pltpu.CompilerParams(vmem_limit_bytes=48 * 2**20),
    )(*inputs)


def shards(tokens, ln_gain, ln_bias, w_attn, b_qv, w_proj, b_proj, w_fc, b_fc, w_out, b_out, d_out):
    parts = block(tokens, d_out, ln_gain, ln_bias, b_proj, b_out, w_attn, b_qv, w_proj, w_fc, b_fc, w_out)
    return tuple(finish(*parts))


def solution(mesh):
    in_specs = (
        P(("dp", "heads"), "width"),
        P(None, "width"),
        P(None, "width"),
        P(None, "width", "heads"),
        P(None, "heads"),
        P("heads", "width"),
        P("width"),
        P("width", "heads"),
        P("heads"),
        P("heads", "width"),
        P("width"),
        P(("dp", "heads"), "width"),
    )
    out_specs = (
        P(("dp", "heads"), "width"),
        P(("dp", "heads"), "width"),
        P(None, "width"),
        P(None, "width"),
        P(None, "width", "heads"),
        P(None, "heads"),
        P("heads", "width"),
        P("width"),
        P("width", "heads"),
        P("heads"),
        P("heads", "width"),
        P("width"),
    )
    return jax.shard_map(shards, mesh=mesh, in_specs=in_specs, out_specs=out_specs, check_vma=False)
```

time: 852 us -> 232 us (0.27)
  waiting for transfers between devices: 432 us -> 0 us
  Pallas kernels: 0 us -> 214 us
  blocking collectives: 144 us -> 0 us
  matrix products: 98.4 us -> 0 us
  other arithmetic: 61.8 us -> 0 us
  local copies, waits for them, and re-layouts: 58.9 us -> 15.7 us
  starting transfers between devices: 37 us -> 0 us
  between operations: 14.8 us -> 0.68 us
    reduce_scatter x4 -> x0, waiting for transfers between devices: 242 us -> none  [sum_width(): lax.psum_scatter(partial_term(jnp.int32(0), row_count * lax.axis_size('wi...]
    pallas_call x0 -> x2, Pallas kernels: none -> 214 us  [the longest x1 211 us: block(): pl.pallas_call(block_kernel, name='block', out_shape=(jax.ShapeDtypeStruc...]
    all_to_all x7 -> x0, blocking collectives: 119 us -> none  [the longest x5 76.4 us: copy_for_each(): return lax.all_to_all(copies, axis, split_axis=0, concat_axis=0, tiled=True)]
    dot_general x18 -> x0, matrix products: 98.4 us -> none  [the longest x4 17.6 us: dot_rows(): return jnp.dot(left_side, right_side, preferred_element_type=jnp.float32)]
    all_to_all x8 -> x0, waiting for transfers between devices: 84.4 us -> none  [the longest x5 60.5 us: copy_for_each(): return lax.all_to_all(copies, axis, split_axis=0, concat_axis=0, tiled=True)]
    all_gather x4 -> x0, waiting for transfers between devices: 71.9 us -> none  [width_rows(): return lax.all_gather(local_part, 'width', axis=0, tiled=True)]
    convert_element_type x16 -> x0, other arithmetic: 36.1 us -> none  [the longest x1 14.6 us: one_block(): grad_scores = (normalized * (grad_probs - row_inner)).astype(jnp.bfloat16)]
    all_to_all x8 -> x0, starting transfers between devices: 35.7 us -> none  [the longest x5 22.2 us: copy_for_each(): return lax.all_to_all(copies, axis, split_axis=0, concat_axis=0, tiled=True)]
  transfers between devices with their start and end apart: 17 -> 0, of which waited for: 13 -> 0; matrix products, arithmetic and copies ran while one was open for 17% -> 0% of each run, Pallas kernels for 0% -> 0%
where the time goes in v2:
time: 232 us; the launch traced here: 230 us
  Pallas kernels  214 us (92%)
  local copies, waits for them, and re-layouts  15.7 us (7%)
    pallas_call x1, Pallas kernels, block(): pl.pallas_call(block_kernel, name='block', out_shape=(jax.ShapeDtypeStruc...  211 us
    unnamed x19, local copies, waits for them, and re-layouts  12.2 us

profile of v2, /device:TPU:0, one launch (start us, length us, event | category | flops | bytes accessed | tf_op | source)
XLA Modules:
  0.0 230.2 jit_solution(5160716449656288858)
XLA Ops:
  0.6 0.0 copy-start.7
  0.7 2.0 copy.24.refs_0_
  2.6 1.9 copy.25.refs_1_
  4.5 0.0 copy-done.7
  4.5 1.3 copy.26.refs_11_
  5.8 211.3 %block.1 = (bf16[4,128,320]{2,1,0:T(8,128)(2,1)}, bf16[4,128,320]{2,1,0:T(8,128)(2,1)}, bf16[320,1280]{1,0:T(8,128)(2,1)}, bf16[320,1280]{1,0:T(8,128)(2,1)}, bf...) custom-call(bf16[512,320]{1,0:T(8,128)(2,1)} %copy.24.refs_0_, ...), custom_call_target="tpu_custom_call" | custom-call | tf_op jit(solution)/shard_map/block/pallas_call | solution.py:787
  217.1 0.0 copy-start
  217.1 1.1 copy-done
  218.2 0.0 copy-start.1
  218.2 1.1 copy-done.1
  219.4 0.0 copy-start.2
  219.4 1.0 copy-done.2
  220.4 0.0 copy-start.3
  220.4 1.0 copy-done.3
  221.4 0.0 copy-start.4
  221.4 1.0 copy-done.4
  222.4 0.0 copy-start.5
  222.4 1.0 copy-done.5
  223.4 0.0 copy-start.6
  223.4 0.8 copy-done.6
  224.2 2.5 %finish.1 = (bf16[512,320]{1,0:T(8,128)(2,1)S(1)}, bf16[512,320]{1,0:T(8,128)(2,1)S(1)}, f32[2,320]{1,0:T(2,128)}, f32[2,320]{1,0:T(2,128)}, f32[3,320,320]{2,1,...) custom-call(bf16[4,128,320]{2,1,0:T(8,128)(2,1)S(1)} %copy-done.4, ...), custom_call_target="tpu_custom_call" | custom-call | tf_op jit(solution)/shard_map/finish/pallas_call | solution.py:845
  226.7 0.9 copy.27
  227.6 0.9 copy.28
  228.5 1.7 copy.29
Async XLA Ops:
  0.6 3.9 %copy-start.7 = (bf16[1280,320]{0,1:T(8,128)(2,1)S(1)}, bf16[1280,320]{0,1:T(8,128)(2,1)}, u32[]{:S(2)}) copy-start(bf16[1280,320]{0,1:T(8,128)(2,1)} %param.21) | copy-start | bytes 2457604
  217.1 1.1 copy-start
  218.2 1.1 copy-start.1
  219.4 1.0 copy-start.2
  220.4 1.0 copy-start.3
  221.4 1.0 copy-start.4
  222.4 1.0 copy-start.5
  223.4 0.8 copy-start.6
